TPU v7x, 32 devices: a whole 2x2x4 slice. The times are simulated.
32 devices in a mesh: grp: 2 (over x), lat: 16 (over z, y, core).
Axes of the slice: x: 2, y: 2, z: 4, core: 2. Of those that a mesh axis runs over, the one named last changes fastest.
Arguments:
- grid_values: bfloat16 [32, 64, 304], P('grp', None, 'lat'), parts along dimension 0, may hold values from -6 to 6
- quad_weights: float32 [128], replicated, may hold values from 0.5 to 4
- owner_map: int32 [512], replicated, may hold values from 0 to 15, as said below
- legendre: bfloat16 [512, 512, 128], P('lat'), may hold values from -0.5 to 0.5
- diffusion: float32 [4], replicated, may hold values from 1 to 16
Outputs:
- grid_result: bfloat16 [32, 64, 304], P('grp', None, 'lat'), parts along dimension 0
There are 2 independent parts, one for each index of `grp`. A program takes and returns all parts, laid end to end along the dimension named above; an argument that names none is the same for every part. Nothing has to cross between parts.
Inputs may be any that keep to these rules, and one draw needn't show every extreme that they name: `owner_map`: every index of lat owns exactly 32 wavenumbers; m and 511 - m have the same owner.
All inputs are finite; a program needn't handle non-finite values.
Results may differ from a plain program's by a relative error of at most 0.007.
Values may be sent and summed in bfloat16 or wider, within the bound.
No kernel may reach another device: no remote copies, remote signals or barrier semaphores. Data moves between devices by JAX's collectives and lax.ppermute only.
A program may use at most 128 MiB of HBM per device.

v0:
```python
import functools
import math

import jax
import jax.numpy as jnp
from jax import lax
from jax.experimental import pallas as pl
from jax.experimental.pallas import tpu as pltpu
from jax.sharding import PartitionSpec as P

LEVELS = 4


TWO_PI = 2.0 * math.pi


def pair_rows(lat_total):
    half = lat_total // 2
    quarter = lat_total // 4
    pair_ids = jnp.arange(half, dtype=jnp.int32)
    north = pair_ids < quarter
    shifted = pair_ids - quarter
    first = jnp.where(north, pair_ids, half + shifted)
    second = jnp.where(north, half - 1 - pair_ids, lat_total - 1 - shifted)
    return (first, second)


def row_length(lat_ids, lat_total):
    return 20 + 4 * jnp.minimum(lat_ids, lat_total - 1 - lat_ids)


def trig_table(length, offset, col_count, wave_ids):
    col_ids = jnp.arange(col_count, dtype=jnp.int32)
    local = col_ids - offset
    phases = local[:, None] * wave_ids[None, :] % length
    angles = phases.astype(jnp.float32) / length.astype(jnp.float32) * TWO_PI
    usable = (local[:, None] >= 0) & (local[:, None] < length) & (2 * wave_ids[None, :] < length)
    cos_part = jnp.where(usable, jnp.cos(angles), 0.0).astype(jnp.bfloat16)
    sin_part = jnp.where(usable, jnp.sin(angles), 0.0).astype(jnp.bfloat16)
    return jnp.concatenate([cos_part, sin_part], axis=1)


def any_rows_body(grid_values, quad_weights, owner_map, legendre, diffusion):
    channels, half_total, col_dev = grid_values.shape
    groups = lax.axis_size("lat")
    device = lax.axis_index("lat")
    half_dev = half_total // groups
    lat_total = 2 * half_total
    row_width = col_dev * groups
    owned_slots = legendre.shape[0]
    wave_count = legendre.shape[1]
    wave_ids = jnp.arange(wave_count, dtype=jnp.int32)
    slot_order = jnp.argsort(owner_map, stable=True)
    inverse_order = jnp.argsort(slot_order)
    my_waves = lax.dynamic_slice_in_dim(slot_order, device * owned_slots, owned_slots)
    contract = (((0,), (1,)), ((), ()))
    first, second = pair_rows(lat_total)
    my_first = lax.dynamic_slice_in_dim(first, device * half_dev, half_dev)
    my_second = lax.dynamic_slice_in_dim(second, device * half_dev, half_dev)
    first_len = row_length(my_first, lat_total)
    second_len = row_length(my_second, lat_total)
    first_weight = jnp.take(quad_weights, my_first)
    second_weight = jnp.take(quad_weights, my_second)

    def pair_tables(packed):
        len_a, len_b = packed
        return jnp.concatenate(
            [
                trig_table(len_a, 0, row_width, wave_ids),
                trig_table(len_b, len_a, row_width, wave_ids),
            ],
            axis=1,
        )

    all_tables = lax.map(pair_tables, (first_len, second_len))

    def forward_pair(row_data, tables):
        totals = lax.dot_general(tables, row_data, contract, preferred_element_type=jnp.float32)
        return (totals[: 2 * wave_count], totals[2 * wave_count :])

    def inverse_pair(coeffs_a, coeffs_b, tables):
        joined = jnp.concatenate([coeffs_a, coeffs_b], axis=0)
        return lax.dot_general(joined, tables, contract, preferred_element_type=jnp.float32).astype(
            jnp.bfloat16
        )

    def scaled(totals, weight, length):
        row_scale = weight / length.astype(jnp.float32)
        return jnp.concatenate(
            [totals[:wave_count] * row_scale, totals[wave_count:] * -row_scale], axis=0
        ).astype(jnp.bfloat16)

    def forward_one_pair(packed):
        row_data, tables, len_a, len_b, weight_a, weight_b = packed
        totals_a, totals_b = forward_pair(row_data, tables)
        return jnp.stack([scaled(totals_a, weight_a, len_a), scaled(totals_b, weight_b, len_b)])

    per_pair = lax.map(
        forward_one_pair,
        (
            jnp.moveaxis(
                lax.all_to_all(grid_values, "lat", split_axis=1, concat_axis=2, tiled=True), 1, 0
            ),
            all_tables,
            first_len,
            second_len,
            first_weight,
            second_weight,
        ),
    )
    per_lat = per_pair.transpose(1, 0, 2, 3).reshape(2 * half_dev, 2, wave_count, -1)
    fourier = per_lat.transpose(2, 1, 3, 0)
    picked = fourier[slot_order]
    rates = jnp.repeat(diffusion, LEVELS)
    degree = jnp.arange(wave_count, dtype=jnp.int32)
    ladder = (degree * (degree + 1)).astype(jnp.float32)
    factor = 1.0 / (1.0 + rates[:, None] * (ladder[None, :] / float(wave_count * (wave_count - 1))))
    damping = jnp.where((degree[None, :] >= my_waves[:, None])[:, None, :], factor[None, :, :], 0.0)
    spectral = jnp.einsum(
        "snl,spcl->spcn",
        legendre,
        lax.all_to_all(picked, "lat", split_axis=0, concat_axis=3, tiled=True),
        preferred_element_type=jnp.float32,
    )
    filtered = (spectral * damping[:, None, :, :]).astype(jnp.bfloat16)
    back = jnp.einsum("snl,spcn->spcl", legendre, filtered, preferred_element_type=jnp.float32)
    returned = back.astype(jnp.bfloat16)
    double = jnp.where(wave_ids == 0, 1.0, 2.0).astype(jnp.bfloat16)
    by_wave = lax.all_to_all(returned, "lat", split_axis=3, concat_axis=0, tiled=True)[
        inverse_order
    ]
    real_part = by_wave[:, 0] * double[:, None, None]
    imag_part = -(by_wave[:, 1] * double[:, None, None])
    stacked = jnp.concatenate([real_part, imag_part], axis=0)

    def backward_one_pair(packed):
        coeffs_a, coeffs_b, tables, len_a, len_b = packed
        return inverse_pair(coeffs_a, coeffs_b, tables)

    per_pair = lax.map(
        backward_one_pair,
        (
            jnp.moveaxis(stacked[:, :, :half_dev], 2, 0),
            jnp.moveaxis(stacked[:, :, half_dev:], 2, 0),
            all_tables,
            first_len,
            second_len,
        ),
    )
    rows_out = jnp.moveaxis(per_pair, 0, 1)
    return lax.all_to_all(rows_out, "lat", split_axis=2, concat_axis=1, tiled=True)


SIN_POLY = (3.141592640130707, -5.1677100835078775, 2.550077523214437, -0.5982912856197345, 0.07765766030450941)
COS_POLY = (0.9999999532476085, -4.934792830619644, 4.058411352862619, -1.3318765680811142, 0.2196896110983216)
LANES = 128
SUB = 8
HOPS = (0, 1, 2, 3)
SUM_ORDER = (3, 1, 2, 0)
GATHER_ORDER = (1, 2, 3)
F32 = jnp.float32
BF16 = jnp.bfloat16


def horner(poly, u):
    total = poly[-1]
    for term in poly[-2::-1]:
        total = total * u + term
    return total


def iota(shape, axis):
    return lax.broadcasted_iota(jnp.int32, shape, axis)


def swap_blocks(v):
    sub = iota(v.shape, 1)
    lane = iota(v.shape, 2)
    for bit in range(3):
        step = 1 << bit
        row_bit = (sub >> bit) & 1
        lane_bit = (lane >> (3 + bit)) & 1
        up = pltpu.roll(pltpu.roll(v, SUB - step, 1), SUB * step, 2)
        down = pltpu.roll(pltpu.roll(v, step, 1), LANES - SUB * step, 2)
        v = jnp.where(row_bit == lane_bit, v, jnp.where(row_bit == 0, up, down))
    return v


def pack_kernel(x_ref, o_ref):
    cols, channels, rows = x_ref.shape
    half = channels // 2
    x = x_ref[...].astype(F32)
    v = swap_blocks(jnp.concatenate([x[:, :half], x[:, half:]], axis=2))
    o_ref[...] = v.reshape(cols * SUB, LANES).astype(BF16)


def unpack_kernel(*refs):
    o_ref = refs[-1]
    cols, channels, rows = o_ref.shape
    half = channels // 2
    total = refs[0][...].astype(F32)
    for x_ref in refs[1:-1]:
        total = total + x_ref[...].astype(F32)
    v = swap_blocks(total.reshape(cols, SUB, LANES))
    o_ref[:, :half] = v[:, :, :rows].astype(BF16)
    o_ref[:, half:] = v[:, :, rows:].astype(BF16)


def join_kernel(order, x_ref, y_ref, *o_refs):
    for i, o_ref in zip(order, o_refs):
        o_ref[...] = (x_ref[i].astype(F32) + y_ref[i].astype(F32)).astype(BF16)


def end_kernel(i, x_ref, y_ref, z_ref, o_ref):
    o_ref[...] = (x_ref[i].astype(F32) + y_ref[i].astype(F32) + z_ref[...].astype(F32)).astype(BF16)


def row_lengths(r, half_total):
    quarter = half_total // 2
    lat_total = 2 * half_total
    north = r < quarter
    first = jnp.where(north, r, half_total + r - quarter)
    second = jnp.where(north, half_total - 1 - r, lat_total - 1 - (r - quarter))
    return row_length(first, lat_total), row_length(second, lat_total)


def table_kernel(half_total, cols, waves, device_ref, owner_ref, tt_ref, wave_ref, jf_ref):
    points = tt_ref.shape[1]
    slots = wave_ref.shape[0]
    line = points // (4 * cols)
    device = device_ref[0]
    low = waves // 2
    owned = jnp.where(owner_ref[:, :low] == device, 1.0, 0.0)
    owned = jnp.broadcast_to(owned, (LANES, low)).T
    below = jnp.where(iota((low, low), 1) <= iota((low, low), 0), 1.0, 0.0).astype(BF16)
    count = jnp.dot(below, owned.astype(BF16), preferred_element_type=F32)
    wave_id = iota((low, LANES), 0).astype(F32)
    lane_slot = (iota((low, LANES), 1) % slots).astype(F32)
    hit = (owned > 0.5) & (count - 1.0 == lane_slot)
    wave = jnp.sum(jnp.where(hit, wave_id, 0.0), axis=0, keepdims=True)
    wave_ref[...] = jnp.broadcast_to(wave, (LANES, LANES)).T[:slots]
    place = iota((points, LANES), 0)
    origin = jnp.floor((place.astype(F32) + 0.5) * (1.0 / cols)).astype(jnp.int32)
    rest = place - origin * cols
    part = origin // line
    line_id = origin - part * line
    part = jnp.where(part < 2, 2 * part + 1, 2 * part - 4)
    hop = sum(jnp.where(line_id == i, HOPS[i], 0) for i in range(1, line))
    step = hop * 4 + (part & 1) * 2 + part // 2
    column = (device ^ step) * cols + rest
    jf_ref[...] = column.astype(F32)

    def block(t, carry):
        r = SUB * t + iota((1, LANES), 1) // slots
        len_a, len_b = row_lengths(r, half_total)
        len_a = len_a.astype(F32)
        len_b = len_b.astype(F32)
        inv_a = 1.0 / len_a
        inv_b = 1.0 / len_b
        end_a = jnp.where(2.0 * wave < len_a, len_a, 0.0)
        end_b = jnp.where(2.0 * wave < len_b, len_a + len_b, 0.0)
        for chunk in range(points // 16):
            span = slice(16 * chunk, 16 * chunk + 16)
            jf = jf_ref[span]
            in_a = jf < len_a
            length = jnp.where(in_a, len_a, len_b)
            inverse = jnp.where(in_a, inv_a, inv_b)
            phase = jnp.where(in_a, jf, jf - len_a) * wave
            turns = jnp.floor(phase * inverse + 0.5)
            part = (phase - turns * length) * inverse
            square = part * part
            half_sin = part * horner(SIN_POLY, square)
            half_cos = horner(COS_POLY, square)
            cos_part = 1.0 - 2.0 * (half_sin * half_sin)
            sin_part = 2.0 * (half_sin * half_cos)
            use_a = jf < end_a
            use_b = (jf < end_b) & jnp.logical_not(in_a)
            tt_ref[t, span, 0:LANES] = jnp.where(use_a, cos_part, 0.0).astype(BF16)
            tt_ref[t, span, LANES : 2 * LANES] = jnp.where(use_a, sin_part, 0.0).astype(BF16)
            tt_ref[t, span, 2 * LANES : 3 * LANES] = jnp.where(use_b, cos_part, 0.0).astype(BF16)
            tt_ref[t, span, 3 * LANES : 4 * LANES] = jnp.where(use_b, sin_part, 0.0).astype(BF16)
        return carry

    lax.fori_loop(0, half_total // SUB, block, 0)


def turn_kernel(half_total, tt_ref, weight_ref, rate_ref, tr_ref, scale_ref, factor_ref):
    lat_total = 2 * half_total
    waves = factor_ref.shape[0]

    def block(t, carry):
        for i in range(4):
            lanes = slice(i * LANES, (i + 1) * LANES)
            tr_ref[t, lanes, :] = tt_ref[t, :, lanes].T
        return carry

    lax.fori_loop(0, half_total // SUB, block, 0)
    weight = jnp.broadcast_to(weight_ref[...], (LANES, lat_total)).T
    scale = weight / row_length(iota((lat_total, LANES), 0), lat_total).astype(F32)
    keep = iota((SUB, LANES), 1) % SUB == iota((SUB, LANES), 0)
    quarter = half_total // 2
    for t in range(half_total // SUB):
        r = SUB * t
        if r < quarter:
            first, second = r, half_total - 1 - r
        else:
            first, second = half_total + r - quarter, lat_total - 1 - (r - quarter)
        under = scale[second - SUB + 1 : second + 1]
        under = jnp.concatenate([under[SUB - 1 - i : SUB - i] for i in range(SUB)], axis=0)
        scale_ref[2 * t] = jnp.where(keep, scale[first : first + SUB], 0.0)
        scale_ref[2 * t + 1] = jnp.where(keep, under, 0.0)
    fields = rate_ref.shape[1]
    field = iota((1, LANES), 1) % (LANES // SUB) // LEVELS
    rate = jnp.zeros((1, LANES), F32)
    for i in range(fields):
        rate = jnp.where(field == i, rate_ref[:, i : i + 1], rate)
    degree = iota((waves, LANES), 0)
    ladder = (degree * (degree + 1)).astype(F32) / float(waves * (waves - 1))
    factor_ref[...] = 1.0 / (1.0 + rate * ladder)


def main_kernel(
    x0_ref, x1_ref, x2_ref, x3_ref, tt_ref, tr_ref, wave_ref, scale_ref, factor_ref, leg_ref, o1_ref, o3_ref, rhs_ref, z_ref, at_ref, bt_ref
):
    blocks, points, _ = tt_ref.shape
    slots, waves, lat_total = leg_ref.shape
    line, lines, _ = x0_ref.shape
    for i, x_ref in enumerate((x1_ref, x3_ref, x0_ref, x2_ref)):
        for j in range(line):
            z_ref[(i * line + j) * lines : (i * line + j + 1) * lines] = x_ref[j].astype(F32)
    row2 = iota((2 * LANES, LANES), 0)
    col2 = iota((2 * LANES, LANES), 1)
    gather = jnp.where(row2 // SUB == col2, jnp.where(row2 < LANES, 1.0, -1.0), 0.0).astype(BF16)
    row3 = iota((LANES, 2 * LANES), 0)
    col3 = iota((LANES, 2 * LANES), 1)
    spread = jnp.where(col3 // SUB == row3, jnp.where(col3 < LANES, 1.0, -1.0), 0.0).astype(BF16)
    slab = SUB * slots // 2

    def forward(t, carry):
        z = z_ref[pl.ds(t, points, stride=SUB), :].astype(BF16)
        d = jnp.dot(tr_ref[t], z, preferred_element_type=F32)
        for h in range(2):
            parts = []
            for p in range(2):
                base = (2 * h + p) * LANES
                rows = [
                    d[base + i * slots : base + (i + 1) * slots] * scale_ref[2 * t + h, i : i + 1, :]
                    for i in range(SUB)
                ]
                parts.append(jnp.concatenate(rows, axis=0).astype(BF16))
            a = jnp.dot(jnp.concatenate(parts, axis=1), gather, preferred_element_type=F32)
            for i in range(2):
                at_ref[pl.ds(pl.multiple_of((2 * t + i) * LANES + h * slab, SUB), slab), :] = a[i * slab : (i + 1) * slab]
        return carry

    lax.fori_loop(0, blocks, forward, 0, unroll=8)
    degree = iota((waves, LANES), 0).astype(F32)

    def slot(s, carry):
        f = at_ref[pl.ds(s, lat_total, stride=slots), :].astype(BF16)
        table = leg_ref[s]
        spectral = jnp.dot(table, f, preferred_element_type=F32)
        wave = wave_ref[pl.ds(s, 1), :]
        kept = jnp.where(degree >= wave, spectral * factor_ref[...], 0.0).astype(BF16)
        back = lax.dot_general(table, kept, (((0,), (0,)), ((), ())), preferred_element_type=F32)
        back = back.astype(BF16).astype(F32) * jnp.where(wave == 0.0, 1.0, 2.0)
        bt_ref[pl.ds(s, lat_total, stride=slots), :] = back
        return carry

    lax.fori_loop(0, slots, slot, 0, unroll=16)
    reach = -(points // 2) // 16 * -16
    keep = (iota((LANES, 2 * LANES), 1) % SUB) == iota((LANES, 2 * LANES), 0) // slots

    def inverse(t, carry):
        rhs = []
        for h in range(2):
            b = jnp.concatenate(
                [bt_ref[pl.ds(pl.multiple_of((2 * t + i) * LANES + h * slab, SUB), slab), :] for i in range(2)], axis=0
            ).astype(BF16)
            wide = jnp.dot(b, spread, preferred_element_type=F32)
            wide = jnp.where(keep, wide, 0.0).astype(BF16)
            rhs.append(wide[:, :LANES])
            rhs.append(wide[:, LANES:])
        rhs = jnp.concatenate(rhs, axis=0)
        rhs_ref[t] = rhs
        out = jnp.dot(tt_ref[t, :reach], rhs, preferred_element_type=F32)
        z_ref[pl.ds(t, points // 2, stride=SUB), :] = out[: points // 2]
        return carry

    lax.fori_loop(0, blocks, inverse, 0, unroll=8)
    for i, o_ref in enumerate((o1_ref, o3_ref)):
        for j in range(line):
            o_ref[j] = z_ref[(i * line + j) * lines : (i * line + j + 1) * lines].astype(BF16)


def near_kernel(tt_ref, rhs_ref, o0_ref, o2_ref, z_ref):
    blocks, points, _ = tt_ref.shape
    line, lines, _ = o0_ref.shape
    from_row = points // 2 // 16 * 16

    def inverse(t, carry):
        out = jnp.dot(tt_ref[t, from_row:], rhs_ref[t], preferred_element_type=F32)
        z_ref[pl.ds(t, points // 2, stride=SUB), :] = out[points // 2 - from_row :]
        return carry

    lax.fori_loop(0, blocks, inverse, 0, unroll=8)
    for i, o_ref in enumerate((o0_ref, o2_ref)):
        for j in range(line):
            o_ref[j] = z_ref[(i * line + j) * lines : (i * line + j + 1) * lines].astype(BF16)


def kernel_call(body, out_shape, in_specs, scratch=(), flops=0, moved=0):
    return pl.pallas_call(
        body,
        out_shape=out_shape,
        in_specs=in_specs,
        scratch_shapes=list(scratch),
        compiler_params=pltpu.CompilerParams(vmem_limit_bytes=12 << 20),
        cost_estimate=pl.CostEstimate(flops=flops, bytes_accessed=moved, transcendentals=0),
    )


def transform_call(parts, tt, tr, wave, scale, factor, legendre):
    slots = wave.shape[0]
    waves, lat_total = legendre.shape[1:]
    line, lines, _ = parts[0].shape
    whole = pl.BlockSpec(memory_space=pltpu.VMEM)
    return pl.pallas_call(
        main_kernel,
        out_shape=[jax.ShapeDtypeStruct((line, lines, LANES), BF16)] * 2
        + [jax.ShapeDtypeStruct(tt.shape[:1] + (4 * LANES, LANES), BF16)],
        in_specs=[whole] * 10,
        out_specs=[whole] * 3,
        scratch_shapes=[
            pltpu.VMEM((4 * line * lines, LANES), F32),
            pltpu.VMEM((lat_total * slots, LANES), F32),
            pltpu.VMEM((lat_total * slots, LANES), F32),
        ],
        compiler_params=pltpu.CompilerParams(vmem_limit_bytes=16 << 20),
    )(*parts, tt, tr, wave, scale, factor, legendre)


def short_rows_body(grid_values, quad_weights, owner_map, legendre, diffusion):
    channels, half_total, cols = grid_values.shape
    groups = lax.axis_size("lat")
    line = groups // 4
    device = lax.axis_index("lat").astype(jnp.int32)
    waves = legendre.shape[1]
    lat_total = legendre.shape[2]
    slots = legendre.shape[0] // 2
    blocks = half_total // SUB
    points = cols * groups
    lines = cols * SUB
    whole = pl.BlockSpec(memory_space=pltpu.VMEM)
    shape = jax.ShapeDtypeStruct
    with jax.named_scope("pack"):
        mine = kernel_call(pack_kernel, shape((lines, LANES), BF16), [whole])(jnp.transpose(grid_values, (2, 0, 1)))

    def across(x, step):
        return lax.ppermute(x, "lat", [(i, i ^ step) for i in range(groups)])

    with jax.named_scope("gather_line"):
        arrived = {hop: across(mine, 4 * hop) for hop in GATHER_ORDER}
        arrived = [arrived[hop] for hop in HOPS[1:]]
    with jax.named_scope("tables"):
        tt, wave = kernel_call(
            functools.partial(table_kernel, half_total, cols, waves),
            (shape((blocks, points, 4 * LANES), BF16), shape((slots, LANES), F32)),
            [pl.BlockSpec(memory_space=pltpu.SMEM), whole],
            [pltpu.VMEM((points, LANES), F32)],
            flops=12 << 20,
            moved=3 << 20,
        )(device[None], owner_map[None, :])
        arrived, tt, wave = lax.optimization_barrier((arrived, tt, wave))
    with jax.named_scope("gather_line"):
        p0 = jnp.stack([mine] + arrived)
    with jax.named_scope("gather_plane"):
        p1 = across(p0, 2)
        tr, scale, factor = kernel_call(
            functools.partial(turn_kernel, half_total),
            (
                shape((blocks, 4 * LANES, points), BF16),
                shape((2 * blocks, SUB, LANES), F32),
                shape((waves, LANES), F32),
            ),
            [whole, whole, whole],
            flops=12 << 20,
            moved=6 << 20,
        )(tt, quad_weights[None, :], diffusion[None, :])
        half_legendre = legendre[:slots]
        p1, tr, scale, factor, half_legendre = lax.optimization_barrier((p1, tr, scale, factor, half_legendre))
        p2 = across(p0, 1)
        p3 = across(p1, 1)
    with jax.named_scope("transform"):
        s1, s3, rhs = transform_call((p0, p1, p2, p3), tt, tr, wave, scale, factor, half_legendre)
    block = shape((line, lines, LANES), BF16)
    with jax.named_scope("sum_cores"):
        r3 = across(s3, 1)
        s0, s2 = kernel_call(near_kernel, [block] * 2, [whole] * 2, [pltpu.VMEM((2 * line * lines, LANES), F32)])(tt, rhs)
        one = shape((lines, LANES), BF16)
        sums = kernel_call(functools.partial(join_kernel, SUM_ORDER), [one] * line, [whole] * 2)(s1, r3)
        r2 = across(s2, 1)
    with jax.named_scope("sum_plane"):
        sums = [across(piece, 2) for piece in sums]
    with jax.named_scope("sum_line"):
        ready = []
        for i, piece in zip(SUM_ORDER, sums):
            end = kernel_call(functools.partial(end_kernel, i), one, [whole] * 3)(s0, r2, piece)
            ready.append(across(end, 4 * HOPS[i]) if i else end)
    with jax.named_scope("unpack"):
        out = kernel_call(unpack_kernel, shape((cols, channels, half_total), BF16), [whole] * line)(*ready)
    return jnp.transpose(out, (1, 2, 0))


def body(grid_values, quad_weights, owner_map, legendre, diffusion):
    channels, half_total, cols = grid_values.shape
    slots, waves, lat_total = legendre.shape
    groups = lax.axis_size("lat")
    longest = 20 + 4 * (half_total - 1)
    short = (
        longest <= waves
        and groups >= 8
        and groups & (groups - 1) == 0
        and half_total % groups == 0
        and half_total // groups * 2 == SUB
        and groups == 4 * len(HOPS)
        and channels * SUB == LANES
        and channels * half_total == SUB * LANES
        and slots * SUB == 2 * LANES
        and lat_total == LANES
        and cols * groups % 16 == 0
    )
    if short:
        return short_rows_body(grid_values, quad_weights, owner_map, legendre, diffusion)
    return any_rows_body(grid_values, quad_weights, owner_map, legendre, diffusion)


def solution(mesh):
    return jax.shard_map(
        body,
        mesh=mesh,
        in_specs=(P("grp", None, "lat"), P(), P(), P("lat", None, None), P()),
        out_specs=P("grp", None, "lat"),
        check_vma=False,
    )
```

profile of v0, /device:TPU:0, one launch (start us, length us, event | category | flops | bytes accessed | tf_op | source)
XLA Modules:
  0.0 38.1 jit_solution(11331902887530146875)
XLA Ops:
  0.0 0.9 %copy-done = bf16[16,64,19]{1,0,2:T(8,128)(2,1)S(1)} copy-done((bf16[16,64,19]{1,0,2:T(8,128)(2,1)S(1)}, bf16[16,64,19]{1,0,2:T(8,128)(2,1)}, u32[]{:S(2)}) %copy-start) | copy-done | bytes 38936
  1.3 5.1 %collective-permute-start.2 = (bf16[152,128]{1,0:T(8,128)(2,1)S(1)}, bf16[152,128]{1,0:T(8,128)(2,1)S(1)}, u32[]{:S(2)}, u32[]{:S(2)}) collective-permute-start(bf16[152,128]{1,0:T(8,128)(2,1)S(1)} %pack.1), channel_id=1, source_target_pairs={{0,12},{1,13},{2,14},{3,15},{4,8},{5,9},{6,10},{7,11},{8,4},{9,5},... | collective-permute-start | bytes 116744 | tf_op jit(solution)/shard_map/gather_line/ppermute | solution.py:460
  6.4 0.6 %collective-permute-start = (bf16[152,128]{1,0:T(8,128)(2,1)S(1)}, bf16[152,128]{1,0:T(8,128)(2,1)S(1)}, u32[]{:S(2)}, u32[]{:S(2)}) collective-permute-start(bf16[152,128]{1,0:T(8,128)(2,1)S(1)} %pack.1), channel_id=1, source_target_pairs={{0,4},{1,5},{2,6},{3,7},{4,0},{5,1},{6,2},{7,3},{8,12},{9,13},{10,... | collective-permute-start | bytes 116744 | tf_op jit(solution)/shard_map/gather_line/ppermute | solution.py:460
  7.0 0.7 %copy-done.3 = s32[512]{0:T(512)S(1)} copy-done((s32[512]{0:T(512)S(1)}, s32[512]{0:T(512)}, u32[]{:S(2)}) %copy-start.3) | copy-done | bytes 2072
  7.7 2.5 %tables.1 = (bf16[8,304,512]{2,1,0:T(8,128)(2,1)S(1)}, f32[16,128]{1,0:T(8,128)S(1)}) custom-call(s32[1]{0:T(128)} %bitcast.1.device_ref, s32[1,512]{1,0:T(1,128)S(1)} %bitcast.14), custom_call_target="tpu_custom_call" | custom-call | flops 12582912 | bytes 3145728 | tf_op jit(solution)/shard_map/tables/pallas_call | solution.py:466
  10.2 1.0 %collective-permute-done.1 = bf16[152,128]{1,0:T(8,128)(2,1)S(1)} collective-permute-done((bf16[152,128]{1,0:T(8,128)(2,1)S(1)}, bf16[152,128]{1,0:T(8,128)(2,1)S(1)}, u32[]{:S(2)}, u32[]{:S(2)}) %collective-permute-start.1) | collective-permute-done | bytes 38944 | tf_op jit(solution)/shard_map/gather_line/ppermute | solution.py:460
  11.3 1.6 %collective-permute-start.3 = (bf16[4,152,128]{2,1,0:T(8,128)(2,1)S(1)}, bf16[4,152,128]{2,1,0:T(8,128)(2,1)S(1)}, u32[]{:S(2)}, u32[]{:S(2)}) collective-permute-start(bf16[4,152,128]{2,1,0:T(8,128)(2,1)S(1)} %pad_maximum_fusion.x0_ref), channel_id=1, source_target_pairs={{0,2},{1,3},{2,0},{3,1},{4,6},{5,7},{6,4},{7,5},{8,10},{9,11},{10,... | collective-permute-start | bytes 466952 | tf_op jit(solution)/shard_map/gather_plane/ppermute | solution.py:460
  12.9 1.8 %slice.3.leg_ref = bf16[16,512,128]{2,1,0:T(8,128)(2,1)S(1)} slice(bf16[32,512,128]{2,1,0:T(8,128)(2,1)} %param.8), slice={[0:16], [0:512], [0:128]} | slice | bytes 4194304 | tf_op jit(solution)/shard_map/gather_plane/slice | solution.py:490
  14.8 1.4 %gather_plane.1 = (bf16[8,512,304]{2,1,0:T(8,128)(2,1)S(1)}, f32[16,8,128]{2,1,0:T(8,128)S(1)}, f32[512,128]{1,0:T(8,128)S(1)}) custom-call(bf16[8,304,512]{2,1,0:T(8,128)(2,1)S(1)} %get-tuple-element.31.tt_ref, f32[1,128]{1,0:T(1,128)S(1)} %bitcast.12, f32[1,4]{1,0:T(1,128)S(1)} %bitcast.13), custom_call_target="tpu_custom_call" | custom-call | flops 12582912 | bytes 6291456 | tf_op jit(solution)/shard_map/gather_plane/pallas_call | solution.py:479
  16.2 0.4 %collective-permute-done.3.x1_ref = bf16[4,152,128]{2,1,0:T(8,128)(2,1)S(1)} collective-permute-done((bf16[4,152,128]{2,1,0:T(8,128)(2,1)S(1)}, bf16[4,152,128]{2,1,0:T(8,128)(2,1)S(1)}, u32[]{:S(2)}, u32[]{:S(2)}) %collective-permute-start.3) | collective-permute-done | bytes 155680 | tf_op jit(solution)/shard_map/gather_plane/ppermute | solution.py:460
  16.7 1.2 %collective-permute-done.5.x3_ref = bf16[4,152,128]{2,1,0:T(8,128)(2,1)S(1)} collective-permute-done((bf16[4,152,128]{2,1,0:T(8,128)(2,1)S(1)}, bf16[4,152,128]{2,1,0:T(8,128)(2,1)S(1)}, u32[]{:S(2)}, u32[]{:S(2)}) %collective-permute-start.5) | collective-permute-done | bytes 155680 | tf_op jit(solution)/shard_map/gather_plane/ppermute | solution.py:460
  18.0 5.6 %transform.1 = (bf16[4,152,128]{2,1,0:T(8,128)(2,1)S(1)}, bf16[4,152,128]{2,1,0:T(8,128)(2,1)S(1)}, bf16[8,512,128]{2,1,0:T(8,128)(2,1)S(1)}) custom-call(bf16[4,152,128]{2,1,0:T(8,128)(2,1)S(1)} %pad_maximum_fusion.x0_ref, bf16[4,152,128]{2,1,0:T(8,128)(2,1)S(1)} %collective-permute-done.3.x1_ref, bf16[4,152,128]{2,1,0:T(8,128)(2,1)S(1)} %collective-permute-done.4.x2_ref, ...), custom_call_target="tpu_custom_call" | custom-call | tf_op jit(solution)/shard_map/transform/pallas_call | solution.py:428
  23.8 0.5 %sum_cores.2 = (bf16[4,152,128]{2,1,0:T(8,128)(2,1)S(1)}, bf16[4,152,128]{2,1,0:T(8,128)(2,1)S(1)}) custom-call(bf16[8,304,512]{2,1,0:T(8,128)(2,1)S(1)} %get-tuple-element.31.tt_ref, bf16[8,512,128]{2,1,0:T(8,128)(2,1)S(1)} %get-tuple-element.44.rhs_ref), custom_call_target="tpu_custom_call" | custom-call | tf_op jit(solution)/shard_map/sum_cores/pallas_call | solution.py:499
  24.3 0.4 %collective-permute-start.6 = (bf16[4,152,128]{2,1,0:T(8,128)(2,1)S(1)}, bf16[4,152,128]{2,1,0:T(8,128)(2,1)S(1)}, u32[]{:S(2)}, u32[]{:S(2)}) collective-permute-start(bf16[4,152,128]{2,1,0:T(8,128)(2,1)S(1)} %get-tuple-element.46), channel_id=1, source_target_pairs={{0,1},{1,0},{2,3},{3,2},{4,5},{5,4},{6,7},{7,6},{8,9},{9,8},{10,11... | collective-permute-start | bytes 466952 | tf_op jit(solution)/shard_map/sum_cores/ppermute | solution.py:460
  25.0 1.6 %collective-permute-start.8 = (bf16[152,128]{1,0:T(8,128)(2,1)S(1)}, bf16[152,128]{1,0:T(8,128)(2,1)S(1)}, u32[]{:S(2)}, u32[]{:S(2)}) collective-permute-start(bf16[152,128]{1,0:T(8,128)(2,1)S(1)} %get-tuple-element.49), channel_id=1, source_target_pairs={{0,2},{1,3},{2,0},{3,1},{4,6},{5,7},{6,4},{7,5},{8,10},{9,11},{10,... | collective-permute-start | bytes 116744 | tf_op jit(solution)/shard_map/sum_plane/ppermute | solution.py:460
  26.6 0.5 %collective-permute-start.10 = (bf16[152,128]{1,0:T(8,128)(2,1)S(1)}, bf16[152,128]{1,0:T(8,128)(2,1)S(1)}, u32[]{:S(2)}, u32[]{:S(2)}) collective-permute-start(bf16[152,128]{1,0:T(8,128)(2,1)S(1)} %get-tuple-element.50), channel_id=1, source_target_pairs={{0,2},{1,3},{2,0},{3,1},{4,6},{5,7},{6,4},{7,5},{8,10},{9,11},{10,... | collective-permute-start | bytes 116744 | tf_op jit(solution)/shard_map/sum_plane/ppermute | solution.py:460
  27.1 1.5 %collective-permute-start.12 = (bf16[152,128]{1,0:T(8,128)(2,1)S(1)}, bf16[152,128]{1,0:T(8,128)(2,1)S(1)}, u32[]{:S(2)}, u32[]{:S(2)}) collective-permute-start(bf16[152,128]{1,0:T(8,128)(2,1)S(1)} %get-tuple-element.51), channel_id=1, source_target_pairs={{0,2},{1,3},{2,0},{3,1},{4,6},{5,7},{6,4},{7,5},{8,10},{9,11},{10,... | collective-permute-start | bytes 116744 | tf_op jit(solution)/shard_map/sum_plane/ppermute | solution.py:460
  28.7 0.5 %collective-permute-start.14 = (bf16[152,128]{1,0:T(8,128)(2,1)S(1)}, bf16[152,128]{1,0:T(8,128)(2,1)S(1)}, u32[]{:S(2)}, u32[]{:S(2)}) collective-permute-start(bf16[152,128]{1,0:T(8,128)(2,1)S(1)} %get-tuple-element.52), channel_id=1, source_target_pairs={{0,2},{1,3},{2,0},{3,1},{4,6},{5,7},{6,4},{7,5},{8,10},{9,11},{10,... | collective-permute-start | bytes 116744 | tf_op jit(solution)/shard_map/sum_plane/ppermute | solution.py:460
  29.2 2.8 %collective-permute-start.9 = (bf16[152,128]{1,0:T(8,128)(2,1)S(1)}, bf16[152,128]{1,0:T(8,128)(2,1)S(1)}, u32[]{:S(2)}, u32[]{:S(2)}) collective-permute-start(bf16[152,128]{1,0:T(8,128)(2,1)S(1)} %sum_line.4), channel_id=1, source_target_pairs={{0,12},{1,13},{2,14},{3,15},{4,8},{5,9},{6,10},{7,11},{8,4},{9,5},... | collective-permute-start | bytes 116744 | tf_op jit(solution)/shard_map/sum_line/ppermute | solution.py:460
  32.2 2.0 %collective-permute-start.13 = (bf16[152,128]{1,0:T(8,128)(2,1)S(1)}, bf16[152,128]{1,0:T(8,128)(2,1)S(1)}, u32[]{:S(2)}, u32[]{:S(2)}) collective-permute-start(bf16[152,128]{1,0:T(8,128)(2,1)S(1)} %sum_line.6), channel_id=1, source_target_pairs={{0,8},{1,9},{2,10},{3,11},{4,12},{5,13},{6,14},{7,15},{8,0},{9,1},... | collective-permute-start | bytes 116744 | tf_op jit(solution)/shard_map/sum_line/ppermute | solution.py:460
  34.2 0.9 %collective-permute-done.9.refs_0_ = bf16[152,128]{1,0:T(8,128)(2,1)S(1)} collective-permute-done((bf16[152,128]{1,0:T(8,128)(2,1)S(1)}, bf16[152,128]{1,0:T(8,128)(2,1)S(1)}, u32[]{:S(2)}, u32[]{:S(2)}) %collective-permute-start.9) | collective-permute-done | bytes 38944 | tf_op jit(solution)/shard_map/sum_line/ppermute | solution.py:460
  35.1 1.0 %collective-permute-done.11.refs_1_ = bf16[152,128]{1,0:T(8,128)(2,1)S(1)} collective-permute-done((bf16[152,128]{1,0:T(8,128)(2,1)S(1)}, bf16[152,128]{1,0:T(8,128)(2,1)S(1)}, u32[]{:S(2)}, u32[]{:S(2)}) %collective-permute-start.11) | collective-permute-done | bytes 38944 | tf_op jit(solution)/shard_map/sum_line/ppermute | solution.py:460
  36.1 1.0 %collective-permute-done.13.refs_2_ = bf16[152,128]{1,0:T(8,128)(2,1)S(1)} collective-permute-done((bf16[152,128]{1,0:T(8,128)(2,1)S(1)}, bf16[152,128]{1,0:T(8,128)(2,1)S(1)}, u32[]{:S(2)}, u32[]{:S(2)}) %collective-permute-start.13) | collective-permute-done | bytes 38944 | tf_op jit(solution)/shard_map/sum_line/ppermute | solution.py:460
  37.1 1.0 %unpack.1 = bf16[19,16,64]{2,1,0:T(8,128)(2,1)} custom-call(bf16[152,128]{1,0:T(8,128)(2,1)S(1)} %collective-permute-done.9.refs_0_, bf16[152,128]{1,0:T(8,128)(2,1)S(1)} %collective-permute-done.11.refs_1_, bf16[152,128]{1,0:T(8,128)(2,1)S(1)} %collective-permute-done.13.refs_2_, bf16[152,128]{1,0:T(8,128)(2,1)S(1)} %sum_line.7.refs_3_), custom_call_target="tpu_custom_call" | custom-call | tf_op jit(solution)/shard_map/unpack/pallas_call | solution.py:511
  (27 shorter events, 1.3 us)
Async XLA Ops:
  0.0 14.7 %copy-start.2 = (f32[4]{0:T(128)S(1)}, f32[4]{0:T(128)}, u32[]{:S(2)}) copy-start(f32[4]{0:T(128)} %param.9) | copy-start | bytes 52
  0.0 14.7 %copy-start.1 = (f32[128]{0:T(128)S(1)}, f32[128]{0:T(128)}, u32[]{:S(2)}) copy-start(f32[128]{0:T(128)} %param.6) | copy-start | bytes 1540
  0.0 0.9 %copy-start = (bf16[16,64,19]{1,0,2:T(8,128)(2,1)S(1)}, bf16[16,64,19]{1,0,2:T(8,128)(2,1)}, u32[]{:S(2)}) copy-start(bf16[16,64,19]{1,0,2:T(8,128)(2,1)} %param.5) | copy-start | bytes 116740
  1.3 9.0 %collective-permute-start.2 = (bf16[152,128]{1,0:T(8,128)(2,1)S(1)}, bf16[152,128]{1,0:T(8,128)(2,1)S(1)}, u32[]{:S(2)}, u32[]{:S(2)}) collective-permute-start(bf16[152,128]{1,0:T(8,128)(2,1)S(1)} %pack.1), channel_id=1, source_target_pairs={{0,12},{1,13},{2,14},{3,15},{4,8},{5,9},{6,10},{7,11},{8,4},{9,5},... | collective-permute-start | bytes 116744 | tf_op jit(solution)/shard_map/gather_line/ppermute | solution.py:460
  6.4 4.9 %collective-permute-start.1 = (bf16[152,128]{1,0:T(8,128)(2,1)S(1)}, bf16[152,128]{1,0:T(8,128)(2,1)S(1)}, u32[]{:S(2)}, u32[]{:S(2)}) collective-permute-start(bf16[152,128]{1,0:T(8,128)(2,1)S(1)} %pack.1), channel_id=1, source_target_pairs={{0,8},{1,9},{2,10},{3,11},{4,12},{5,13},{6,14},{7,15},{8,0},{9,1},... | collective-permute-start | bytes 116744 | tf_op jit(solution)/shard_map/gather_line/ppermute | solution.py:460
  6.4 4.9 %collective-permute-start = (bf16[152,128]{1,0:T(8,128)(2,1)S(1)}, bf16[152,128]{1,0:T(8,128)(2,1)S(1)}, u32[]{:S(2)}, u32[]{:S(2)}) collective-permute-start(bf16[152,128]{1,0:T(8,128)(2,1)S(1)} %pack.1), channel_id=1, source_target_pairs={{0,4},{1,5},{2,6},{3,7},{4,0},{5,1},{6,2},{7,3},{8,12},{9,13},{10,... | collective-permute-start | bytes 116744 | tf_op jit(solution)/shard_map/gather_line/ppermute | solution.py:460
  7.0 0.7 %copy-start.3 = (s32[512]{0:T(512)S(1)}, s32[512]{0:T(512)}, u32[]{:S(2)}) copy-start(s32[512]{0:T(512)} %param.7) | copy-start | bytes 6148
  11.3 5.3 %collective-permute-start.3 = (bf16[4,152,128]{2,1,0:T(8,128)(2,1)S(1)}, bf16[4,152,128]{2,1,0:T(8,128)(2,1)S(1)}, u32[]{:S(2)}, u32[]{:S(2)}) collective-permute-start(bf16[4,152,128]{2,1,0:T(8,128)(2,1)S(1)} %pad_maximum_fusion.x0_ref), channel_id=1, source_target_pairs={{0,2},{1,3},{2,0},{3,1},{4,6},{5,7},{6,4},{7,5},{8,10},{9,11},{10,... | collective-permute-start | bytes 466952 | tf_op jit(solution)/shard_map/gather_plane/ppermute | solution.py:460
  14.7 2.1 %collective-permute-start.4 = (bf16[4,152,128]{2,1,0:T(8,128)(2,1)S(1)}, bf16[4,152,128]{2,1,0:T(8,128)(2,1)S(1)}, u32[]{:S(2)}, u32[]{:S(2)}) collective-permute-start(bf16[4,152,128]{2,1,0:T(8,128)(2,1)S(1)} %pad_maximum_fusion.x0_ref), channel_id=1, source_target_pairs={{0,1},{1,0},{2,3},{3,2},{4,5},{5,4},{6,7},{7,6},{8,9},{9,8},{10,11... | collective-permute-start | bytes 466952 | tf_op jit(solution)/shard_map/gather_plane/ppermute | solution.py:460
  16.6 1.4 %collective-permute-start.5 = (bf16[4,152,128]{2,1,0:T(8,128)(2,1)S(1)}, bf16[4,152,128]{2,1,0:T(8,128)(2,1)S(1)}, u32[]{:S(2)}, u32[]{:S(2)}) collective-permute-start(bf16[4,152,128]{2,1,0:T(8,128)(2,1)S(1)} %collective-permute-done.3.x1_ref), channel_id=1, source_target_pairs={{0,1},{1,0},{2,3},{3,2},{4,5},{5,4},{6,7},{7,6},{8,9},{9,8},{10,11... | collective-permute-start | bytes 466952 | tf_op jit(solution)/shard_map/gather_plane/ppermute | solution.py:460
  23.5 1.4 %collective-permute-start.7 = (bf16[4,152,128]{2,1,0:T(8,128)(2,1)S(1)}, bf16[4,152,128]{2,1,0:T(8,128)(2,1)S(1)}, u32[]{:S(2)}, u32[]{:S(2)}) collective-permute-start(bf16[4,152,128]{2,1,0:T(8,128)(2,1)S(1)} %get-tuple-element.48), channel_id=1, source_target_pairs={{0,1},{1,0},{2,3},{3,2},{4,5},{5,4},{6,7},{7,6},{8,9},{9,8},{10,11... | collective-permute-start | bytes 466952 | tf_op jit(solution)/shard_map/sum_cores/ppermute | solution.py:460
  24.3 4.9 %collective-permute-start.6 = (bf16[4,152,128]{2,1,0:T(8,128)(2,1)S(1)}, bf16[4,152,128]{2,1,0:T(8,128)(2,1)S(1)}, u32[]{:S(2)}, u32[]{:S(2)}) collective-permute-start(bf16[4,152,128]{2,1,0:T(8,128)(2,1)S(1)} %get-tuple-element.46), channel_id=1, source_target_pairs={{0,1},{1,0},{2,3},{3,2},{4,5},{5,4},{6,7},{7,6},{8,9},{9,8},{10,11... | collective-permute-start | bytes 466952 | tf_op jit(solution)/shard_map/sum_cores/ppermute | solution.py:460
  25.0 4.1 %collective-permute-start.8 = (bf16[152,128]{1,0:T(8,128)(2,1)S(1)}, bf16[152,128]{1,0:T(8,128)(2,1)S(1)}, u32[]{:S(2)}, u32[]{:S(2)}) collective-permute-start(bf16[152,128]{1,0:T(8,128)(2,1)S(1)} %get-tuple-element.49), channel_id=1, source_target_pairs={{0,2},{1,3},{2,0},{3,1},{4,6},{5,7},{6,4},{7,5},{8,10},{9,11},{10,... | collective-permute-start | bytes 116744 | tf_op jit(solution)/shard_map/sum_plane/ppermute | solution.py:460
  26.6 5.4 %collective-permute-start.10 = (bf16[152,128]{1,0:T(8,128)(2,1)S(1)}, bf16[152,128]{1,0:T(8,128)(2,1)S(1)}, u32[]{:S(2)}, u32[]{:S(2)}) collective-permute-start(bf16[152,128]{1,0:T(8,128)(2,1)S(1)} %get-tuple-element.50), channel_id=1, source_target_pairs={{0,2},{1,3},{2,0},{3,1},{4,6},{5,7},{6,4},{7,5},{8,10},{9,11},{10,... | collective-permute-start | bytes 116744 | tf_op jit(solution)/shard_map/sum_plane/ppermute | solution.py:460
  27.1 5.0 %collective-permute-start.12 = (bf16[152,128]{1,0:T(8,128)(2,1)S(1)}, bf16[152,128]{1,0:T(8,128)(2,1)S(1)}, u32[]{:S(2)}, u32[]{:S(2)}) collective-permute-start(bf16[152,128]{1,0:T(8,128)(2,1)S(1)} %get-tuple-element.51), channel_id=1, source_target_pairs={{0,2},{1,3},{2,0},{3,1},{4,6},{5,7},{6,4},{7,5},{8,10},{9,11},{10,... | collective-permute-start | bytes 116744 | tf_op jit(solution)/shard_map/sum_plane/ppermute | solution.py:460
  28.7 5.6 %collective-permute-start.14 = (bf16[152,128]{1,0:T(8,128)(2,1)S(1)}, bf16[152,128]{1,0:T(8,128)(2,1)S(1)}, u32[]{:S(2)}, u32[]{:S(2)}) collective-permute-start(bf16[152,128]{1,0:T(8,128)(2,1)S(1)} %get-tuple-element.52), channel_id=1, source_target_pairs={{0,2},{1,3},{2,0},{3,1},{4,6},{5,7},{6,4},{7,5},{8,10},{9,11},{10,... | collective-permute-start | bytes 116744 | tf_op jit(solution)/shard_map/sum_plane/ppermute | solution.py:460
  29.2 5.9 %collective-permute-start.9 = (bf16[152,128]{1,0:T(8,128)(2,1)S(1)}, bf16[152,128]{1,0:T(8,128)(2,1)S(1)}, u32[]{:S(2)}, u32[]{:S(2)}) collective-permute-start(bf16[152,128]{1,0:T(8,128)(2,1)S(1)} %sum_line.4), channel_id=1, source_target_pairs={{0,12},{1,13},{2,14},{3,15},{4,8},{5,9},{6,10},{7,11},{8,4},{9,5},... | collective-permute-start | bytes 116744 | tf_op jit(solution)/shard_map/sum_line/ppermute | solution.py:460
  32.1 4.0 %collective-permute-start.11 = (bf16[152,128]{1,0:T(8,128)(2,1)S(1)}, bf16[152,128]{1,0:T(8,128)(2,1)S(1)}, u32[]{:S(2)}, u32[]{:S(2)}) collective-permute-start(bf16[152,128]{1,0:T(8,128)(2,1)S(1)} %sum_line.5), channel_id=1, source_target_pairs={{0,4},{1,5},{2,6},{3,7},{4,0},{5,1},{6,2},{7,3},{8,12},{9,13},{10,... | collective-permute-start | bytes 116744 | tf_op jit(solution)/shard_map/sum_line/ppermute | solution.py:460
  32.2 4.9 %collective-permute-start.13 = (bf16[152,128]{1,0:T(8,128)(2,1)S(1)}, bf16[152,128]{1,0:T(8,128)(2,1)S(1)}, u32[]{:S(2)}, u32[]{:S(2)}) collective-permute-start(bf16[152,128]{1,0:T(8,128)(2,1)S(1)} %sum_line.6), channel_id=1, source_target_pairs={{0,8},{1,9},{2,10},{3,11},{4,12},{5,13},{6,14},{7,15},{8,0},{9,1},... | collective-permute-start | bytes 116744 | tf_op jit(solution)/shard_map/sum_line/ppermute | solution.py:460
where the time goes:
time: 38.3 us; the launch traced here: 38.1 us
  starting transfers between devices  17.3 us (45%)
  Pallas kernels  11.5 us (30%)
  waiting for transfers between devices  5.84 us (15%)
  local copies, waits for them, and re-layouts  3.38 us (9%)
    ppermute x15, starting transfers between devices, across(): return lax.ppermute(x, 'lat', [(i, i ^ step) for i in range(groups)])  17.3 us
    ppermute x15, waiting for transfers between devices, across(): return lax.ppermute(x, 'lat', [(i, i ^ step) for i in range(groups)])  5.84 us
    pallas_call x1, Pallas kernels, transform_call(): pl.pallas_call(main_kernel, out_shape=[jax.ShapeDtypeStruct((line, lines,...  5.58 us
    pallas_call x1, Pallas kernels, short_rows_body(): kernel_call(functools.partial(table_kernel, half_total, cols, waves), (sh...  2.53 us
    slice x1, local copies, waits for them, and re-layouts, short_rows_body(): half_legendre = legendre[:slots]  1.78 us
    unnamed x8, local copies, waits for them, and re-layouts  1.6 us
    pallas_call x1, Pallas kernels, short_rows_body(): kernel_call(functools.partial(turn_kernel, half_total), (shape((blocks, 4...  1.41 us
    pallas_call x1, Pallas kernels, short_rows_body(): kernel_call(unpack_kernel, shape((cols, channels, half_total), BF16), [wh...  0.99 us
  transfers between devices with their start and end apart: 15, of which 7 were waited for; matrix products, arithmetic and copies ran while one was open for 5% of the time, Pallas kernels for 12%

commit v1 on v0

--- a/solution.py
+++ b/solution.py
@@ -151,8 +151,8 @@
     return lax.all_to_all(rows_out, "lat", split_axis=2, concat_axis=1, tiled=True)
 
 
-SIN_POLY = (3.141592640130707, -5.1677100835078775, 2.550077523214437, -0.5982912856197345, 0.07765766030450941)
-COS_POLY = (0.9999999532476085, -4.934792830619644, 4.058411352862619, -1.3318765680811142, 0.2196896110983216)
+SIN_POLY = (4.44288291912434, -7.30824568650904, 3.60635421843265, -0.846111650373064, 0.1098245164248)
+COS_POLY = (1.41421349625523, -6.97885094856382, 5.73946037690726, -1.88355790598724, 0.310688027527717)
 LANES = 128
 SUB = 8
 HOPS = (0, 1, 2, 3)
@@ -255,24 +255,21 @@
         len_a, len_b = row_lengths(r, half_total)
         len_a = len_a.astype(F32)
         len_b = len_b.astype(F32)
-        inv_a = 1.0 / len_a
-        inv_b = 1.0 / len_b
+        rate_a = wave / len_a
+        rate_b = wave / len_b
         end_a = jnp.where(2.0 * wave < len_a, len_a, 0.0)
         end_b = jnp.where(2.0 * wave < len_b, len_a + len_b, 0.0)
         for chunk in range(points // 16):
             span = slice(16 * chunk, 16 * chunk + 16)
             jf = jf_ref[span]
             in_a = jf < len_a
-            length = jnp.where(in_a, len_a, len_b)
-            inverse = jnp.where(in_a, inv_a, inv_b)
-            phase = jnp.where(in_a, jf, jf - len_a) * wave
-            turns = jnp.floor(phase * inverse + 0.5)
-            part = (phase - turns * length) * inverse
+            turns = jnp.where(in_a, jf, jf - len_a) * jnp.where(in_a, rate_a, rate_b)
+            part = turns - jnp.round(turns)
             square = part * part
             half_sin = part * horner(SIN_POLY, square)
             half_cos = horner(COS_POLY, square)
-            cos_part = 1.0 - 2.0 * (half_sin * half_sin)
-            sin_part = 2.0 * (half_sin * half_cos)
+            cos_part = 1.0 - half_sin * half_sin
+            sin_part = half_sin * half_cos
             use_a = jf < end_a
             use_b = (jf < end_b) & jnp.logical_not(in_a)
             tt_ref[t, span, 0:LANES] = jnp.where(use_a, cos_part, 0.0).astype(BF16)

time: 38.3 us -> 38.1 us (level)
  transfers between devices with their start and end apart: 15 -> 15, of which waited for: 7 -> 7; matrix products, arithmetic and copies ran while one was open for 5% -> 5% of each run, Pallas kernels for 12% -> 11%
where the time goes in v1:
time: 38.1 us; the launch traced here: 37.9 us
  starting transfers between devices  17.1 us (45%)
  Pallas kernels  11.2 us (29%)
  waiting for transfers between devices  6.11 us (16%)
  local copies, waits for them, and re-layouts  3.38 us (9%)
    ppermute x15, starting transfers between devices, across(): return lax.ppermute(x, 'lat', [(i, i ^ step) for i in range(groups)])  17.1 us
    ppermute x15, waiting for transfers between devices, across(): return lax.ppermute(x, 'lat', [(i, i ^ step) for i in range(groups)])  6.11 us
    pallas_call x1, Pallas kernels, transform_call(): pl.pallas_call(main_kernel, out_shape=[jax.ShapeDtypeStruct((line, lines,...  5.58 us
    pallas_call x1, Pallas kernels, short_rows_body(): kernel_call(functools.partial(table_kernel, half_total, cols, waves), (sh...  2.26 us
    slice x1, local copies, waits for them, and re-layouts, short_rows_body(): half_legendre = legendre[:slots]  1.78 us
    unnamed x8, local copies, waits for them, and re-layouts  1.6 us
    pallas_call x1, Pallas kernels, short_rows_body(): kernel_call(functools.partial(turn_kernel, half_total), (shape((blocks, 4...  1.41 us
    pallas_call x1, Pallas kernels, short_rows_body(): kernel_call(unpack_kernel, shape((cols, channels, half_total), BF16), [wh...  0.99 us
  transfers between devices with their start and end apart: 15, of which 7 were waited for; matrix products, arithmetic and copies ran while one was open for 5% of the time, Pallas kernels for 11%

profile of v1, /device:TPU:0, one launch (start us, length us, event | category | flops | bytes accessed | tf_op | source)
XLA Modules:
  0.0 37.9 jit_solution(17828232787430373353)
XLA Ops:
  0.0 0.9 %copy-done = bf16[16,64,19]{1,0,2:T(8,128)(2,1)S(1)} copy-done((bf16[16,64,19]{1,0,2:T(8,128)(2,1)S(1)}, bf16[16,64,19]{1,0,2:T(8,128)(2,1)}, u32[]{:S(2)}) %copy-start) | copy-done | bytes 38936
  1.3 5.1 %collective-permute-start.2 = (bf16[152,128]{1,0:T(8,128)(2,1)S(1)}, bf16[152,128]{1,0:T(8,128)(2,1)S(1)}, u32[]{:S(2)}, u32[]{:S(2)}) collective-permute-start(bf16[152,128]{1,0:T(8,128)(2,1)S(1)} %pack.1), channel_id=1, source_target_pairs={{0,12},{1,13},{2,14},{3,15},{4,8},{5,9},{6,10},{7,11},{8,4},{9,5},... | collective-permute-start | bytes 116744 | tf_op jit(solution)/shard_map/gather_line/ppermute | solution.py:457
  6.4 0.6 %collective-permute-start = (bf16[152,128]{1,0:T(8,128)(2,1)S(1)}, bf16[152,128]{1,0:T(8,128)(2,1)S(1)}, u32[]{:S(2)}, u32[]{:S(2)}) collective-permute-start(bf16[152,128]{1,0:T(8,128)(2,1)S(1)} %pack.1), channel_id=1, source_target_pairs={{0,4},{1,5},{2,6},{3,7},{4,0},{5,1},{6,2},{7,3},{8,12},{9,13},{10,... | collective-permute-start | bytes 116744 | tf_op jit(solution)/shard_map/gather_line/ppermute | solution.py:457
  7.0 0.7 %copy-done.3 = s32[512]{0:T(512)S(1)} copy-done((s32[512]{0:T(512)S(1)}, s32[512]{0:T(512)}, u32[]{:S(2)}) %copy-start.3) | copy-done | bytes 2072
  7.7 2.3 %tables.1 = (bf16[8,304,512]{2,1,0:T(8,128)(2,1)S(1)}, f32[16,128]{1,0:T(8,128)S(1)}) custom-call(s32[1]{0:T(128)} %bitcast.1.device_ref, s32[1,512]{1,0:T(1,128)S(1)} %bitcast.14), custom_call_target="tpu_custom_call" | custom-call | flops 12582912 | bytes 3145728 | tf_op jit(solution)/shard_map/tables/pallas_call | solution.py:463
  10.0 1.3 %collective-permute-done.1 = bf16[152,128]{1,0:T(8,128)(2,1)S(1)} collective-permute-done((bf16[152,128]{1,0:T(8,128)(2,1)S(1)}, bf16[152,128]{1,0:T(8,128)(2,1)S(1)}, u32[]{:S(2)}, u32[]{:S(2)}) %collective-permute-start.1) | collective-permute-done | bytes 38944 | tf_op jit(solution)/shard_map/gather_line/ppermute | solution.py:457
  11.3 1.6 %collective-permute-start.3 = (bf16[4,152,128]{2,1,0:T(8,128)(2,1)S(1)}, bf16[4,152,128]{2,1,0:T(8,128)(2,1)S(1)}, u32[]{:S(2)}, u32[]{:S(2)}) collective-permute-start(bf16[4,152,128]{2,1,0:T(8,128)(2,1)S(1)} %pad_maximum_fusion.x0_ref), channel_id=1, source_target_pairs={{0,2},{1,3},{2,0},{3,1},{4,6},{5,7},{6,4},{7,5},{8,10},{9,11},{10,... | collective-permute-start | bytes 466952 | tf_op jit(solution)/shard_map/gather_plane/ppermute | solution.py:457
  12.9 1.8 %slice.3.leg_ref = bf16[16,512,128]{2,1,0:T(8,128)(2,1)S(1)} slice(bf16[32,512,128]{2,1,0:T(8,128)(2,1)} %param.8), slice={[0:16], [0:512], [0:128]} | slice | bytes 4194304 | tf_op jit(solution)/shard_map/gather_plane/slice | solution.py:487
  14.8 1.4 %gather_plane.1 = (bf16[8,512,304]{2,1,0:T(8,128)(2,1)S(1)}, f32[16,8,128]{2,1,0:T(8,128)S(1)}, f32[512,128]{1,0:T(8,128)S(1)}) custom-call(bf16[8,304,512]{2,1,0:T(8,128)(2,1)S(1)} %get-tuple-element.31.tt_ref, f32[1,128]{1,0:T(1,128)S(1)} %bitcast.12, f32[1,4]{1,0:T(1,128)S(1)} %bitcast.13), custom_call_target="tpu_custom_call" | custom-call | flops 12582912 | bytes 6291456 | tf_op jit(solution)/shard_map/gather_plane/pallas_call | solution.py:476
  16.2 0.4 %collective-permute-done.3.x1_ref = bf16[4,152,128]{2,1,0:T(8,128)(2,1)S(1)} collective-permute-done((bf16[4,152,128]{2,1,0:T(8,128)(2,1)S(1)}, bf16[4,152,128]{2,1,0:T(8,128)(2,1)S(1)}, u32[]{:S(2)}, u32[]{:S(2)}) %collective-permute-start.3) | collective-permute-done | bytes 155680 | tf_op jit(solution)/shard_map/gather_plane/ppermute | solution.py:457
  16.7 1.2 %collective-permute-done.5.x3_ref = bf16[4,152,128]{2,1,0:T(8,128)(2,1)S(1)} collective-permute-done((bf16[4,152,128]{2,1,0:T(8,128)(2,1)S(1)}, bf16[4,152,128]{2,1,0:T(8,128)(2,1)S(1)}, u32[]{:S(2)}, u32[]{:S(2)}) %collective-permute-start.5) | collective-permute-done | bytes 155680 | tf_op jit(solution)/shard_map/gather_plane/ppermute | solution.py:457
  18.0 5.6 %transform.1 = (bf16[4,152,128]{2,1,0:T(8,128)(2,1)S(1)}, bf16[4,152,128]{2,1,0:T(8,128)(2,1)S(1)}, bf16[8,512,128]{2,1,0:T(8,128)(2,1)S(1)}) custom-call(bf16[4,152,128]{2,1,0:T(8,128)(2,1)S(1)} %pad_maximum_fusion.x0_ref, bf16[4,152,128]{2,1,0:T(8,128)(2,1)S(1)} %collective-permute-done.3.x1_ref, bf16[4,152,128]{2,1,0:T(8,128)(2,1)S(1)} %collective-permute-done.4.x2_ref, ...), custom_call_target="tpu_custom_call" | custom-call | tf_op jit(solution)/shard_map/transform/pallas_call | solution.py:425
  23.8 0.5 %sum_cores.2 = (bf16[4,152,128]{2,1,0:T(8,128)(2,1)S(1)}, bf16[4,152,128]{2,1,0:T(8,128)(2,1)S(1)}) custom-call(bf16[8,304,512]{2,1,0:T(8,128)(2,1)S(1)} %get-tuple-element.31.tt_ref, bf16[8,512,128]{2,1,0:T(8,128)(2,1)S(1)} %get-tuple-element.44.rhs_ref), custom_call_target="tpu_custom_call" | custom-call | tf_op jit(solution)/shard_map/sum_cores/pallas_call | solution.py:496
  24.3 0.4 %collective-permute-start.6 = (bf16[4,152,128]{2,1,0:T(8,128)(2,1)S(1)}, bf16[4,152,128]{2,1,0:T(8,128)(2,1)S(1)}, u32[]{:S(2)}, u32[]{:S(2)}) collective-permute-start(bf16[4,152,128]{2,1,0:T(8,128)(2,1)S(1)} %get-tuple-element.46), channel_id=1, source_target_pairs={{0,1},{1,0},{2,3},{3,2},{4,5},{5,4},{6,7},{7,6},{8,9},{9,8},{10,11... | collective-permute-start | bytes 466952 | tf_op jit(solution)/shard_map/sum_cores/ppermute | solution.py:457
  25.0 1.6 %collective-permute-start.8 = (bf16[152,128]{1,0:T(8,128)(2,1)S(1)}, bf16[152,128]{1,0:T(8,128)(2,1)S(1)}, u32[]{:S(2)}, u32[]{:S(2)}) collective-permute-start(bf16[152,128]{1,0:T(8,128)(2,1)S(1)} %get-tuple-element.49), channel_id=1, source_target_pairs={{0,2},{1,3},{2,0},{3,1},{4,6},{5,7},{6,4},{7,5},{8,10},{9,11},{10,... | collective-permute-start | bytes 116744 | tf_op jit(solution)/shard_map/sum_plane/ppermute | solution.py:457
  26.6 0.5 %collective-permute-start.10 = (bf16[152,128]{1,0:T(8,128)(2,1)S(1)}, bf16[152,128]{1,0:T(8,128)(2,1)S(1)}, u32[]{:S(2)}, u32[]{:S(2)}) collective-permute-start(bf16[152,128]{1,0:T(8,128)(2,1)S(1)} %get-tuple-element.50), channel_id=1, source_target_pairs={{0,2},{1,3},{2,0},{3,1},{4,6},{5,7},{6,4},{7,5},{8,10},{9,11},{10,... | collective-permute-start | bytes 116744 | tf_op jit(solution)/shard_map/sum_plane/ppermute | solution.py:457
  27.1 1.5 %collective-permute-start.12 = (bf16[152,128]{1,0:T(8,128)(2,1)S(1)}, bf16[152,128]{1,0:T(8,128)(2,1)S(1)}, u32[]{:S(2)}, u32[]{:S(2)}) collective-permute-start(bf16[152,128]{1,0:T(8,128)(2,1)S(1)} %get-tuple-element.51), channel_id=1, source_target_pairs={{0,2},{1,3},{2,0},{3,1},{4,6},{5,7},{6,4},{7,5},{8,10},{9,11},{10,... | collective-permute-start | bytes 116744 | tf_op jit(solution)/shard_map/sum_plane/ppermute | solution.py:457
  28.7 0.5 %collective-permute-start.14 = (bf16[152,128]{1,0:T(8,128)(2,1)S(1)}, bf16[152,128]{1,0:T(8,128)(2,1)S(1)}, u32[]{:S(2)}, u32[]{:S(2)}) collective-permute-start(bf16[152,128]{1,0:T(8,128)(2,1)S(1)} %get-tuple-element.52), channel_id=1, source_target_pairs={{0,2},{1,3},{2,0},{3,1},{4,6},{5,7},{6,4},{7,5},{8,10},{9,11},{10,... | collective-permute-start | bytes 116744 | tf_op jit(solution)/shard_map/sum_plane/ppermute | solution.py:457
  29.2 2.5 %collective-permute-start.9 = (bf16[152,128]{1,0:T(8,128)(2,1)S(1)}, bf16[152,128]{1,0:T(8,128)(2,1)S(1)}, u32[]{:S(2)}, u32[]{:S(2)}) collective-permute-start(bf16[152,128]{1,0:T(8,128)(2,1)S(1)} %sum_line.4), channel_id=1, source_target_pairs={{0,12},{1,13},{2,14},{3,15},{4,8},{5,9},{6,10},{7,11},{8,4},{9,5},... | collective-permute-start | bytes 116744 | tf_op jit(solution)/shard_map/sum_line/ppermute | solution.py:457
  32.0 2.0 %collective-permute-start.13 = (bf16[152,128]{1,0:T(8,128)(2,1)S(1)}, bf16[152,128]{1,0:T(8,128)(2,1)S(1)}, u32[]{:S(2)}, u32[]{:S(2)}) collective-permute-start(bf16[152,128]{1,0:T(8,128)(2,1)S(1)} %sum_line.6), channel_id=1, source_target_pairs={{0,8},{1,9},{2,10},{3,11},{4,12},{5,13},{6,14},{7,15},{8,0},{9,1},... | collective-permute-start | bytes 116744 | tf_op jit(solution)/shard_map/sum_line/ppermute | solution.py:457
  34.0 1.0 %collective-permute-done.9.refs_0_ = bf16[152,128]{1,0:T(8,128)(2,1)S(1)} collective-permute-done((bf16[152,128]{1,0:T(8,128)(2,1)S(1)}, bf16[152,128]{1,0:T(8,128)(2,1)S(1)}, u32[]{:S(2)}, u32[]{:S(2)}) %collective-permute-start.9) | collective-permute-done | bytes 38944 | tf_op jit(solution)/shard_map/sum_line/ppermute | solution.py:457
  35.0 0.8 %collective-permute-done.11.refs_1_ = bf16[152,128]{1,0:T(8,128)(2,1)S(1)} collective-permute-done((bf16[152,128]{1,0:T(8,128)(2,1)S(1)}, bf16[152,128]{1,0:T(8,128)(2,1)S(1)}, u32[]{:S(2)}, u32[]{:S(2)}) %collective-permute-start.11) | collective-permute-done | bytes 38944 | tf_op jit(solution)/shard_map/sum_line/ppermute | solution.py:457
  35.8 1.1 %collective-permute-done.13.refs_2_ = bf16[152,128]{1,0:T(8,128)(2,1)S(1)} collective-permute-done((bf16[152,128]{1,0:T(8,128)(2,1)S(1)}, bf16[152,128]{1,0:T(8,128)(2,1)S(1)}, u32[]{:S(2)}, u32[]{:S(2)}) %collective-permute-start.13) | collective-permute-done | bytes 38944 | tf_op jit(solution)/shard_map/sum_line/ppermute | solution.py:457
  36.9 1.0 %unpack.1 = bf16[19,16,64]{2,1,0:T(8,128)(2,1)} custom-call(bf16[152,128]{1,0:T(8,128)(2,1)S(1)} %collective-permute-done.9.refs_0_, bf16[152,128]{1,0:T(8,128)(2,1)S(1)} %collective-permute-done.11.refs_1_, bf16[152,128]{1,0:T(8,128)(2,1)S(1)} %collective-permute-done.13.refs_2_, bf16[152,128]{1,0:T(8,128)(2,1)S(1)} %sum_line.7.refs_3_), custom_call_target="tpu_custom_call" | custom-call | tf_op jit(solution)/shard_map/unpack/pallas_call | solution.py:508
  (27 shorter events, 1.4 us)
Async XLA Ops:
  0.0 14.7 %copy-start.2 = (f32[4]{0:T(128)S(1)}, f32[4]{0:T(128)}, u32[]{:S(2)}) copy-start(f32[4]{0:T(128)} %param.9) | copy-start | bytes 52
  0.0 14.7 %copy-start.1 = (f32[128]{0:T(128)S(1)}, f32[128]{0:T(128)}, u32[]{:S(2)}) copy-start(f32[128]{0:T(128)} %param.6) | copy-start | bytes 1540
  0.0 0.9 %copy-start = (bf16[16,64,19]{1,0,2:T(8,128)(2,1)S(1)}, bf16[16,64,19]{1,0,2:T(8,128)(2,1)}, u32[]{:S(2)}) copy-start(bf16[16,64,19]{1,0,2:T(8,128)(2,1)} %param.5) | copy-start | bytes 116740
  1.3 8.7 %collective-permute-start.2 = (bf16[152,128]{1,0:T(8,128)(2,1)S(1)}, bf16[152,128]{1,0:T(8,128)(2,1)S(1)}, u32[]{:S(2)}, u32[]{:S(2)}) collective-permute-start(bf16[152,128]{1,0:T(8,128)(2,1)S(1)} %pack.1), channel_id=1, source_target_pairs={{0,12},{1,13},{2,14},{3,15},{4,8},{5,9},{6,10},{7,11},{8,4},{9,5},... | collective-permute-start | bytes 116744 | tf_op jit(solution)/shard_map/gather_line/ppermute | solution.py:457
  6.4 4.9 %collective-permute-start.1 = (bf16[152,128]{1,0:T(8,128)(2,1)S(1)}, bf16[152,128]{1,0:T(8,128)(2,1)S(1)}, u32[]{:S(2)}, u32[]{:S(2)}) collective-permute-start(bf16[152,128]{1,0:T(8,128)(2,1)S(1)} %pack.1), channel_id=1, source_target_pairs={{0,8},{1,9},{2,10},{3,11},{4,12},{5,13},{6,14},{7,15},{8,0},{9,1},... | collective-permute-start | bytes 116744 | tf_op jit(solution)/shard_map/gather_line/ppermute | solution.py:457
  6.4 4.9 %collective-permute-start = (bf16[152,128]{1,0:T(8,128)(2,1)S(1)}, bf16[152,128]{1,0:T(8,128)(2,1)S(1)}, u32[]{:S(2)}, u32[]{:S(2)}) collective-permute-start(bf16[152,128]{1,0:T(8,128)(2,1)S(1)} %pack.1), channel_id=1, source_target_pairs={{0,4},{1,5},{2,6},{3,7},{4,0},{5,1},{6,2},{7,3},{8,12},{9,13},{10,... | collective-permute-start | bytes 116744 | tf_op jit(solution)/shard_map/gather_line/ppermute | solution.py:457
  7.0 0.7 %copy-start.3 = (s32[512]{0:T(512)S(1)}, s32[512]{0:T(512)}, u32[]{:S(2)}) copy-start(s32[512]{0:T(512)} %param.7) | copy-start | bytes 6148
  11.3 5.3 %collective-permute-start.3 = (bf16[4,152,128]{2,1,0:T(8,128)(2,1)S(1)}, bf16[4,152,128]{2,1,0:T(8,128)(2,1)S(1)}, u32[]{:S(2)}, u32[]{:S(2)}) collective-permute-start(bf16[4,152,128]{2,1,0:T(8,128)(2,1)S(1)} %pad_maximum_fusion.x0_ref), channel_id=1, source_target_pairs={{0,2},{1,3},{2,0},{3,1},{4,6},{5,7},{6,4},{7,5},{8,10},{9,11},{10,... | collective-permute-start | bytes 466952 | tf_op jit(solution)/shard_map/gather_plane/ppermute | solution.py:457
  14.7 2.1 %collective-permute-start.4 = (bf16[4,152,128]{2,1,0:T(8,128)(2,1)S(1)}, bf16[4,152,128]{2,1,0:T(8,128)(2,1)S(1)}, u32[]{:S(2)}, u32[]{:S(2)}) collective-permute-start(bf16[4,152,128]{2,1,0:T(8,128)(2,1)S(1)} %pad_maximum_fusion.x0_ref), channel_id=1, source_target_pairs={{0,1},{1,0},{2,3},{3,2},{4,5},{5,4},{6,7},{7,6},{8,9},{9,8},{10,11... | collective-permute-start | bytes 466952 | tf_op jit(solution)/shard_map/gather_plane/ppermute | solution.py:457
  16.6 1.4 %collective-permute-start.5 = (bf16[4,152,128]{2,1,0:T(8,128)(2,1)S(1)}, bf16[4,152,128]{2,1,0:T(8,128)(2,1)S(1)}, u32[]{:S(2)}, u32[]{:S(2)}) collective-permute-start(bf16[4,152,128]{2,1,0:T(8,128)(2,1)S(1)} %collective-permute-done.3.x1_ref), channel_id=1, source_target_pairs={{0,1},{1,0},{2,3},{3,2},{4,5},{5,4},{6,7},{7,6},{8,9},{9,8},{10,11... | collective-permute-start | bytes 466952 | tf_op jit(solution)/shard_map/gather_plane/ppermute | solution.py:457
  23.5 1.4 %collective-permute-start.7 = (bf16[4,152,128]{2,1,0:T(8,128)(2,1)S(1)}, bf16[4,152,128]{2,1,0:T(8,128)(2,1)S(1)}, u32[]{:S(2)}, u32[]{:S(2)}) collective-permute-start(bf16[4,152,128]{2,1,0:T(8,128)(2,1)S(1)} %get-tuple-element.48), channel_id=1, source_target_pairs={{0,1},{1,0},{2,3},{3,2},{4,5},{5,4},{6,7},{7,6},{8,9},{9,8},{10,11... | collective-permute-start | bytes 466952 | tf_op jit(solution)/shard_map/sum_cores/ppermute | solution.py:457
  24.3 4.9 %collective-permute-start.6 = (bf16[4,152,128]{2,1,0:T(8,128)(2,1)S(1)}, bf16[4,152,128]{2,1,0:T(8,128)(2,1)S(1)}, u32[]{:S(2)}, u32[]{:S(2)}) collective-permute-start(bf16[4,152,128]{2,1,0:T(8,128)(2,1)S(1)} %get-tuple-element.46), channel_id=1, source_target_pairs={{0,1},{1,0},{2,3},{3,2},{4,5},{5,4},{6,7},{7,6},{8,9},{9,8},{10,11... | collective-permute-start | bytes 466952 | tf_op jit(solution)/shard_map/sum_cores/ppermute | solution.py:457
  25.0 4.1 %collective-permute-start.8 = (bf16[152,128]{1,0:T(8,128)(2,1)S(1)}, bf16[152,128]{1,0:T(8,128)(2,1)S(1)}, u32[]{:S(2)}, u32[]{:S(2)}) collective-permute-start(bf16[152,128]{1,0:T(8,128)(2,1)S(1)} %get-tuple-element.49), channel_id=1, source_target_pairs={{0,2},{1,3},{2,0},{3,1},{4,6},{5,7},{6,4},{7,5},{8,10},{9,11},{10,... | collective-permute-start | bytes 116744 | tf_op jit(solution)/shard_map/sum_plane/ppermute | solution.py:457
  26.6 5.1 %collective-permute-start.10 = (bf16[152,128]{1,0:T(8,128)(2,1)S(1)}, bf16[152,128]{1,0:T(8,128)(2,1)S(1)}, u32[]{:S(2)}, u32[]{:S(2)}) collective-permute-start(bf16[152,128]{1,0:T(8,128)(2,1)S(1)} %get-tuple-element.50), channel_id=1, source_target_pairs={{0,2},{1,3},{2,0},{3,1},{4,6},{5,7},{6,4},{7,5},{8,10},{9,11},{10,... | collective-permute-start | bytes 116744 | tf_op jit(solution)/shard_map/sum_plane/ppermute | solution.py:457
  27.1 4.8 %collective-permute-start.12 = (bf16[152,128]{1,0:T(8,128)(2,1)S(1)}, bf16[152,128]{1,0:T(8,128)(2,1)S(1)}, u32[]{:S(2)}, u32[]{:S(2)}) collective-permute-start(bf16[152,128]{1,0:T(8,128)(2,1)S(1)} %get-tuple-element.51), channel_id=1, source_target_pairs={{0,2},{1,3},{2,0},{3,1},{4,6},{5,7},{6,4},{7,5},{8,10},{9,11},{10,... | collective-permute-start | bytes 116744 | tf_op jit(solution)/shard_map/sum_plane/ppermute | solution.py:457
  28.7 5.3 %collective-permute-start.14 = (bf16[152,128]{1,0:T(8,128)(2,1)S(1)}, bf16[152,128]{1,0:T(8,128)(2,1)S(1)}, u32[]{:S(2)}, u32[]{:S(2)}) collective-permute-start(bf16[152,128]{1,0:T(8,128)(2,1)S(1)} %get-tuple-element.52), channel_id=1, source_target_pairs={{0,2},{1,3},{2,0},{3,1},{4,6},{5,7},{6,4},{7,5},{8,10},{9,11},{10,... | collective-permute-start | bytes 116744 | tf_op jit(solution)/shard_map/sum_plane/ppermute | solution.py:457
  29.2 5.8 %collective-permute-start.9 = (bf16[152,128]{1,0:T(8,128)(2,1)S(1)}, bf16[152,128]{1,0:T(8,128)(2,1)S(1)}, u32[]{:S(2)}, u32[]{:S(2)}) collective-permute-start(bf16[152,128]{1,0:T(8,128)(2,1)S(1)} %sum_line.4), channel_id=1, source_target_pairs={{0,12},{1,13},{2,14},{3,15},{4,8},{5,9},{6,10},{7,11},{8,4},{9,5},... | collective-permute-start | bytes 116744 | tf_op jit(solution)/shard_map/sum_line/ppermute | solution.py:457
  31.8 4.0 %collective-permute-start.11 = (bf16[152,128]{1,0:T(8,128)(2,1)S(1)}, bf16[152,128]{1,0:T(8,128)(2,1)S(1)}, u32[]{:S(2)}, u32[]{:S(2)}) collective-permute-start(bf16[152,128]{1,0:T(8,128)(2,1)S(1)} %sum_line.5), channel_id=1, source_target_pairs={{0,4},{1,5},{2,6},{3,7},{4,0},{5,1},{6,2},{7,3},{8,12},{9,13},{10,... | collective-permute-start | bytes 116744 | tf_op jit(solution)/shard_map/sum_line/ppermute | solution.py:457
  32.0 4.9 %collective-permute-start.13 = (bf16[152,128]{1,0:T(8,128)(2,1)S(1)}, bf16[152,128]{1,0:T(8,128)(2,1)S(1)}, u32[]{:S(2)}, u32[]{:S(2)}) collective-permute-start(bf16[152,128]{1,0:T(8,128)(2,1)S(1)} %sum_line.6), channel_id=1, source_target_pairs={{0,8},{1,9},{2,10},{3,11},{4,12},{5,13},{6,14},{7,15},{8,0},{9,1},... | collective-permute-start | bytes 116744 | tf_op jit(solution)/shard_map/sum_line/ppermute | solution.py:457

commit v2 on v1

--- a/solution.py
+++ b/solution.py
@@ -157,7 +157,7 @@
 SUB = 8
 HOPS = (0, 1, 2, 3)
 SUM_ORDER = (3, 1, 2, 0)
-GATHER_ORDER = (1, 2, 3)
+GATHER_ORDER = (1, 3, 2)
 F32 = jnp.float32
 BF16 = jnp.bfloat16
 
@@ -197,13 +197,11 @@
 def unpack_kernel(*refs):
     o_ref = refs[-1]
     cols, channels, rows = o_ref.shape
-    half = channels // 2
     total = refs[0][...].astype(F32)
     for x_ref in refs[1:-1]:
         total = total + x_ref[...].astype(F32)
     v = swap_blocks(total.reshape(cols, SUB, LANES))
-    o_ref[:, :half] = v[:, :, :rows].astype(BF16)
-    o_ref[:, half:] = v[:, :, rows:].astype(BF16)
+    o_ref[...] = jnp.concatenate([v[:, :, :rows], v[:, :, rows:]], axis=1).astype(BF16)
 
 
 def join_kernel(order, x_ref, y_ref, *o_refs):
@@ -328,8 +326,9 @@
     row2 = iota((2 * LANES, LANES), 0)
     col2 = iota((2 * LANES, LANES), 1)
     gather = jnp.where(row2 // SUB == col2, jnp.where(row2 < LANES, 1.0, -1.0), 0.0).astype(BF16)
-    row3 = iota((LANES, 2 * LANES), 0)
-    col3 = iota((LANES, 2 * LANES), 1)
+    wide = 2 * LANES // SUB
+    row3 = iota((wide, 2 * LANES), 0)
+    col3 = iota((wide, 2 * LANES), 1)
     spread = jnp.where(col3 // SUB == row3, jnp.where(col3 < LANES, 1.0, -1.0), 0.0).astype(BF16)
     slab = SUB * slots // 2
 
@@ -372,12 +371,12 @@
         rhs = []
         for h in range(2):
             b = jnp.concatenate(
-                [bt_ref[pl.ds(pl.multiple_of((2 * t + i) * LANES + h * slab, SUB), slab), :] for i in range(2)], axis=0
+                [bt_ref[pl.ds(pl.multiple_of((2 * t + i) * LANES + h * slab, SUB), slab), :wide] for i in range(2)], axis=0
             ).astype(BF16)
-            wide = jnp.dot(b, spread, preferred_element_type=F32)
-            wide = jnp.where(keep, wide, 0.0).astype(BF16)
-            rhs.append(wide[:, :LANES])
-            rhs.append(wide[:, LANES:])
+            both = jnp.dot(b, spread, preferred_element_type=F32)
+            both = jnp.where(keep, both, 0.0).astype(BF16)
+            rhs.append(both[:, :LANES])
+            rhs.append(both[:, LANES:])
         rhs = jnp.concatenate(rhs, axis=0)
         rhs_ref[t] = rhs
         out = jnp.dot(tt_ref[t, :reach], rhs, preferred_element_type=F32)
@@ -429,9 +428,9 @@
         in_specs=[whole] * 10,
         out_specs=[whole] * 3,
         scratch_shapes=[
-            pltpu.VMEM((4 * line * lines, LANES), F32),
-            pltpu.VMEM((lat_total * slots, LANES), F32),
-            pltpu.VMEM((lat_total * slots, LANES), F32),
+            pltpu.VMEM((4 * line * lines + SUB, LANES), F32),
+            pltpu.VMEM(((lat_total + 1) * slots, LANES), F32),
+            pltpu.VMEM(((lat_total + 1) * slots, LANES), F32),
         ],
         compiler_params=pltpu.CompilerParams(vmem_limit_bytes=16 << 20),
     )(*parts, tt, tr, wave, scale, factor, legendre)
@@ -493,7 +492,7 @@
     block = shape((line, lines, LANES), BF16)
     with jax.named_scope("sum_cores"):
         r3 = across(s3, 1)
-        s0, s2 = kernel_call(near_kernel, [block] * 2, [whole] * 2, [pltpu.VMEM((2 * line * lines, LANES), F32)])(tt, rhs)
+        s0, s2 = kernel_call(near_kernel, [block] * 2, [whole] * 2, [pltpu.VMEM((2 * line * lines + SUB, LANES), F32)])(tt, rhs)
         one = shape((lines, LANES), BF16)
         sums = kernel_call(functools.partial(join_kernel, SUM_ORDER), [one] * line, [whole] * 2)(s1, r3)
         r2 = across(s2, 1)

time: 38.1 us -> 38.1 us (level)
  no operation moved by 1% of the time
where the time goes in v2:
time: 38.1 us; the launch traced here: 37.9 us
  starting transfers between devices  17 us (45%)
  Pallas kernels  11.2 us (29%)
  waiting for transfers between devices  6.22 us (16%)
  local copies, waits for them, and re-layouts  3.38 us (9%)
    ppermute x15, starting transfers between devices, across(): return lax.ppermute(x, 'lat', [(i, i ^ step) for i in range(groups)])  17 us
    ppermute x15, waiting for transfers between devices, across(): return lax.ppermute(x, 'lat', [(i, i ^ step) for i in range(groups)])  6.22 us
    pallas_call x1, Pallas kernels, transform_call(): pl.pallas_call(main_kernel, out_shape=[jax.ShapeDtypeStruct((line, lines,...  5.55 us
    pallas_call x1, Pallas kernels, short_rows_body(): kernel_call(functools.partial(table_kernel, half_total, cols, waves), (sh...  2.26 us
    slice x1, local copies, waits for them, and re-layouts, short_rows_body(): half_legendre = legendre[:slots]  1.78 us
    unnamed x8, local copies, waits for them, and re-layouts  1.6 us
    pallas_call x1, Pallas kernels, short_rows_body(): kernel_call(functools.partial(turn_kernel, half_total), (shape((blocks, 4...  1.41 us
    pallas_call x1, Pallas kernels, short_rows_body(): kernel_call(unpack_kernel, shape((cols, channels, half_total), BF16), [wh...  0.98 us
  transfers between devices with their start and end apart: 15, of which 7 were waited for; matrix products, arithmetic and copies ran while one was open for 5% of the time, Pallas kernels for 11%

profile of v2, /device:TPU:0, one launch (start us, length us, event | category | flops | bytes accessed | tf_op | source)
XLA Modules:
  0.0 37.9 jit_solution(11726189160791837499)
XLA Ops:
  0.0 0.9 %copy-done = bf16[16,64,19]{1,0,2:T(8,128)(2,1)S(1)} copy-done((bf16[16,64,19]{1,0,2:T(8,128)(2,1)S(1)}, bf16[16,64,19]{1,0,2:T(8,128)(2,1)}, u32[]{:S(2)}) %copy-start) | copy-done | bytes 38936
  1.3 5.1 %collective-permute-start.2 = (bf16[152,128]{1,0:T(8,128)(2,1)S(1)}, bf16[152,128]{1,0:T(8,128)(2,1)S(1)}, u32[]{:S(2)}, u32[]{:S(2)}) collective-permute-start(bf16[152,128]{1,0:T(8,128)(2,1)S(1)} %pack.1), channel_id=1, source_target_pairs={{0,12},{1,13},{2,14},{3,15},{4,8},{5,9},{6,10},{7,11},{8,4},{9,5},... | collective-permute-start | bytes 116744 | tf_op jit(solution)/shard_map/gather_line/ppermute | solution.py:456
  6.4 0.6 %collective-permute-start = (bf16[152,128]{1,0:T(8,128)(2,1)S(1)}, bf16[152,128]{1,0:T(8,128)(2,1)S(1)}, u32[]{:S(2)}, u32[]{:S(2)}) collective-permute-start(bf16[152,128]{1,0:T(8,128)(2,1)S(1)} %pack.1), channel_id=1, source_target_pairs={{0,4},{1,5},{2,6},{3,7},{4,0},{5,1},{6,2},{7,3},{8,12},{9,13},{10,... | collective-permute-start | bytes 116744 | tf_op jit(solution)/shard_map/gather_line/ppermute | solution.py:456
  7.0 0.7 %copy-done.3 = s32[512]{0:T(512)S(1)} copy-done((s32[512]{0:T(512)S(1)}, s32[512]{0:T(512)}, u32[]{:S(2)}) %copy-start.3) | copy-done | bytes 2072
  7.7 2.3 %tables.1 = (bf16[8,304,512]{2,1,0:T(8,128)(2,1)S(1)}, f32[16,128]{1,0:T(8,128)S(1)}) custom-call(s32[1]{0:T(128)} %bitcast.1.device_ref, s32[1,512]{1,0:T(1,128)S(1)} %bitcast.14), custom_call_target="tpu_custom_call" | custom-call | flops 12582912 | bytes 3145728 | tf_op jit(solution)/shard_map/tables/pallas_call | solution.py:462
  10.0 1.3 %collective-permute-done.1 = bf16[152,128]{1,0:T(8,128)(2,1)S(1)} collective-permute-done((bf16[152,128]{1,0:T(8,128)(2,1)S(1)}, bf16[152,128]{1,0:T(8,128)(2,1)S(1)}, u32[]{:S(2)}, u32[]{:S(2)}) %collective-permute-start.1) | collective-permute-done | bytes 38944 | tf_op jit(solution)/shard_map/gather_line/ppermute | solution.py:456
  11.3 1.6 %collective-permute-start.3 = (bf16[4,152,128]{2,1,0:T(8,128)(2,1)S(1)}, bf16[4,152,128]{2,1,0:T(8,128)(2,1)S(1)}, u32[]{:S(2)}, u32[]{:S(2)}) collective-permute-start(bf16[4,152,128]{2,1,0:T(8,128)(2,1)S(1)} %pad_maximum_fusion.x0_ref), channel_id=1, source_target_pairs={{0,2},{1,3},{2,0},{3,1},{4,6},{5,7},{6,4},{7,5},{8,10},{9,11},{10,... | collective-permute-start | bytes 466952 | tf_op jit(solution)/shard_map/gather_plane/ppermute | solution.py:456
  12.9 1.8 %slice.3.leg_ref = bf16[16,512,128]{2,1,0:T(8,128)(2,1)S(1)} slice(bf16[32,512,128]{2,1,0:T(8,128)(2,1)} %param.8), slice={[0:16], [0:512], [0:128]} | slice | bytes 4194304 | tf_op jit(solution)/shard_map/gather_plane/slice | solution.py:486
  14.8 1.4 %gather_plane.1 = (bf16[8,512,304]{2,1,0:T(8,128)(2,1)S(1)}, f32[16,8,128]{2,1,0:T(8,128)S(1)}, f32[512,128]{1,0:T(8,128)S(1)}) custom-call(bf16[8,304,512]{2,1,0:T(8,128)(2,1)S(1)} %get-tuple-element.31.tt_ref, f32[1,128]{1,0:T(1,128)S(1)} %bitcast.12, f32[1,4]{1,0:T(1,128)S(1)} %bitcast.13), custom_call_target="tpu_custom_call" | custom-call | flops 12582912 | bytes 6291456 | tf_op jit(solution)/shard_map/gather_plane/pallas_call | solution.py:475
  16.2 0.4 %collective-permute-done.3.x1_ref = bf16[4,152,128]{2,1,0:T(8,128)(2,1)S(1)} collective-permute-done((bf16[4,152,128]{2,1,0:T(8,128)(2,1)S(1)}, bf16[4,152,128]{2,1,0:T(8,128)(2,1)S(1)}, u32[]{:S(2)}, u32[]{:S(2)}) %collective-permute-start.3) | collective-permute-done | bytes 155680 | tf_op jit(solution)/shard_map/gather_plane/ppermute | solution.py:456
  16.7 1.2 %collective-permute-done.5.x3_ref = bf16[4,152,128]{2,1,0:T(8,128)(2,1)S(1)} collective-permute-done((bf16[4,152,128]{2,1,0:T(8,128)(2,1)S(1)}, bf16[4,152,128]{2,1,0:T(8,128)(2,1)S(1)}, u32[]{:S(2)}, u32[]{:S(2)}) %collective-permute-start.5) | collective-permute-done | bytes 155680 | tf_op jit(solution)/shard_map/gather_plane/ppermute | solution.py:456
  18.0 5.5 %transform.1 = (bf16[4,152,128]{2,1,0:T(8,128)(2,1)S(1)}, bf16[4,152,128]{2,1,0:T(8,128)(2,1)S(1)}, bf16[8,512,128]{2,1,0:T(8,128)(2,1)S(1)}) custom-call(bf16[4,152,128]{2,1,0:T(8,128)(2,1)S(1)} %pad_maximum_fusion.x0_ref, bf16[4,152,128]{2,1,0:T(8,128)(2,1)S(1)} %collective-permute-done.3.x1_ref, bf16[4,152,128]{2,1,0:T(8,128)(2,1)S(1)} %collective-permute-done.4.x2_ref, ...), custom_call_target="tpu_custom_call" | custom-call | tf_op jit(solution)/shard_map/transform/pallas_call | solution.py:424
  23.7 0.5 %sum_cores.2 = (bf16[4,152,128]{2,1,0:T(8,128)(2,1)S(1)}, bf16[4,152,128]{2,1,0:T(8,128)(2,1)S(1)}) custom-call(bf16[8,304,512]{2,1,0:T(8,128)(2,1)S(1)} %get-tuple-element.31.tt_ref, bf16[8,512,128]{2,1,0:T(8,128)(2,1)S(1)} %get-tuple-element.44.rhs_ref), custom_call_target="tpu_custom_call" | custom-call | tf_op jit(solution)/shard_map/sum_cores/pallas_call | solution.py:495
  24.2 0.4 %collective-permute-start.6 = (bf16[4,152,128]{2,1,0:T(8,128)(2,1)S(1)}, bf16[4,152,128]{2,1,0:T(8,128)(2,1)S(1)}, u32[]{:S(2)}, u32[]{:S(2)}) collective-permute-start(bf16[4,152,128]{2,1,0:T(8,128)(2,1)S(1)} %get-tuple-element.46), channel_id=1, source_target_pairs={{0,1},{1,0},{2,3},{3,2},{4,5},{5,4},{6,7},{7,6},{8,9},{9,8},{10,11... | collective-permute-start | bytes 466952 | tf_op jit(solution)/shard_map/sum_cores/ppermute | solution.py:456
  25.0 1.6 %collective-permute-start.8 = (bf16[152,128]{1,0:T(8,128)(2,1)S(1)}, bf16[152,128]{1,0:T(8,128)(2,1)S(1)}, u32[]{:S(2)}, u32[]{:S(2)}) collective-permute-start(bf16[152,128]{1,0:T(8,128)(2,1)S(1)} %get-tuple-element.49), channel_id=1, source_target_pairs={{0,2},{1,3},{2,0},{3,1},{4,6},{5,7},{6,4},{7,5},{8,10},{9,11},{10,... | collective-permute-start | bytes 116744 | tf_op jit(solution)/shard_map/sum_plane/ppermute | solution.py:456
  26.6 0.5 %collective-permute-start.10 = (bf16[152,128]{1,0:T(8,128)(2,1)S(1)}, bf16[152,128]{1,0:T(8,128)(2,1)S(1)}, u32[]{:S(2)}, u32[]{:S(2)}) collective-permute-start(bf16[152,128]{1,0:T(8,128)(2,1)S(1)} %get-tuple-element.50), channel_id=1, source_target_pairs={{0,2},{1,3},{2,0},{3,1},{4,6},{5,7},{6,4},{7,5},{8,10},{9,11},{10,... | collective-permute-start | bytes 116744 | tf_op jit(solution)/shard_map/sum_plane/ppermute | solution.py:456
  27.1 1.5 %collective-permute-start.12 = (bf16[152,128]{1,0:T(8,128)(2,1)S(1)}, bf16[152,128]{1,0:T(8,128)(2,1)S(1)}, u32[]{:S(2)}, u32[]{:S(2)}) collective-permute-start(bf16[152,128]{1,0:T(8,128)(2,1)S(1)} %get-tuple-element.51), channel_id=1, source_target_pairs={{0,2},{1,3},{2,0},{3,1},{4,6},{5,7},{6,4},{7,5},{8,10},{9,11},{10,... | collective-permute-start | bytes 116744 | tf_op jit(solution)/shard_map/sum_plane/ppermute | solution.py:456
  28.6 0.5 %collective-permute-start.14 = (bf16[152,128]{1,0:T(8,128)(2,1)S(1)}, bf16[152,128]{1,0:T(8,128)(2,1)S(1)}, u32[]{:S(2)}, u32[]{:S(2)}) collective-permute-start(bf16[152,128]{1,0:T(8,128)(2,1)S(1)} %get-tuple-element.52), channel_id=1, source_target_pairs={{0,2},{1,3},{2,0},{3,1},{4,6},{5,7},{6,4},{7,5},{8,10},{9,11},{10,... | collective-permute-start | bytes 116744 | tf_op jit(solution)/shard_map/sum_plane/ppermute | solution.py:456
  29.2 2.6 %collective-permute-start.9 = (bf16[152,128]{1,0:T(8,128)(2,1)S(1)}, bf16[152,128]{1,0:T(8,128)(2,1)S(1)}, u32[]{:S(2)}, u32[]{:S(2)}) collective-permute-start(bf16[152,128]{1,0:T(8,128)(2,1)S(1)} %sum_line.4), channel_id=1, source_target_pairs={{0,12},{1,13},{2,14},{3,15},{4,8},{5,9},{6,10},{7,11},{8,4},{9,5},... | collective-permute-start | bytes 116744 | tf_op jit(solution)/shard_map/sum_line/ppermute | solution.py:456
  32.0 1.9 %collective-permute-start.13 = (bf16[152,128]{1,0:T(8,128)(2,1)S(1)}, bf16[152,128]{1,0:T(8,128)(2,1)S(1)}, u32[]{:S(2)}, u32[]{:S(2)}) collective-permute-start(bf16[152,128]{1,0:T(8,128)(2,1)S(1)} %sum_line.6), channel_id=1, source_target_pairs={{0,8},{1,9},{2,10},{3,11},{4,12},{5,13},{6,14},{7,15},{8,0},{9,1},... | collective-permute-start | bytes 116744 | tf_op jit(solution)/shard_map/sum_line/ppermute | solution.py:456
  33.9 1.1 %collective-permute-done.9.refs_0_ = bf16[152,128]{1,0:T(8,128)(2,1)S(1)} collective-permute-done((bf16[152,128]{1,0:T(8,128)(2,1)S(1)}, bf16[152,128]{1,0:T(8,128)(2,1)S(1)}, u32[]{:S(2)}, u32[]{:S(2)}) %collective-permute-start.9) | collective-permute-done | bytes 38944 | tf_op jit(solution)/shard_map/sum_line/ppermute | solution.py:456
  35.0 0.8 %collective-permute-done.11.refs_1_ = bf16[152,128]{1,0:T(8,128)(2,1)S(1)} collective-permute-done((bf16[152,128]{1,0:T(8,128)(2,1)S(1)}, bf16[152,128]{1,0:T(8,128)(2,1)S(1)}, u32[]{:S(2)}, u32[]{:S(2)}) %collective-permute-start.11) | collective-permute-done | bytes 38944 | tf_op jit(solution)/shard_map/sum_line/ppermute | solution.py:456
  35.8 1.1 %collective-permute-done.13.refs_2_ = bf16[152,128]{1,0:T(8,128)(2,1)S(1)} collective-permute-done((bf16[152,128]{1,0:T(8,128)(2,1)S(1)}, bf16[152,128]{1,0:T(8,128)(2,1)S(1)}, u32[]{:S(2)}, u32[]{:S(2)}) %collective-permute-start.13) | collective-permute-done | bytes 38944 | tf_op jit(solution)/shard_map/sum_line/ppermute | solution.py:456
  36.9 1.0 %unpack.1 = bf16[19,16,64]{2,1,0:T(8,128)(2,1)} custom-call(bf16[152,128]{1,0:T(8,128)(2,1)S(1)} %collective-permute-done.9.refs_0_, bf16[152,128]{1,0:T(8,128)(2,1)S(1)} %collective-permute-done.11.refs_1_, bf16[152,128]{1,0:T(8,128)(2,1)S(1)} %collective-permute-done.13.refs_2_, bf16[152,128]{1,0:T(8,128)(2,1)S(1)} %sum_line.7.refs_3_), custom_call_target="tpu_custom_call" | custom-call | tf_op jit(solution)/shard_map/unpack/pallas_call | solution.py:507
  (27 shorter events, 1.4 us)
Async XLA Ops:
  0.0 14.7 %copy-start.2 = (f32[4]{0:T(128)S(1)}, f32[4]{0:T(128)}, u32[]{:S(2)}) copy-start(f32[4]{0:T(128)} %param.9) | copy-start | bytes 52
  0.0 14.7 %copy-start.1 = (f32[128]{0:T(128)S(1)}, f32[128]{0:T(128)}, u32[]{:S(2)}) copy-start(f32[128]{0:T(128)} %param.6) | copy-start | bytes 1540
  0.0 0.9 %copy-start = (bf16[16,64,19]{1,0,2:T(8,128)(2,1)S(1)}, bf16[16,64,19]{1,0,2:T(8,128)(2,1)}, u32[]{:S(2)}) copy-start(bf16[16,64,19]{1,0,2:T(8,128)(2,1)} %param.5) | copy-start | bytes 116740
  1.3 8.7 %collective-permute-start.2 = (bf16[152,128]{1,0:T(8,128)(2,1)S(1)}, bf16[152,128]{1,0:T(8,128)(2,1)S(1)}, u32[]{:S(2)}, u32[]{:S(2)}) collective-permute-start(bf16[152,128]{1,0:T(8,128)(2,1)S(1)} %pack.1), channel_id=1, source_target_pairs={{0,12},{1,13},{2,14},{3,15},{4,8},{5,9},{6,10},{7,11},{8,4},{9,5},... | collective-permute-start | bytes 116744 | tf_op jit(solution)/shard_map/gather_line/ppermute | solution.py:456
  6.4 4.9 %collective-permute-start.1 = (bf16[152,128]{1,0:T(8,128)(2,1)S(1)}, bf16[152,128]{1,0:T(8,128)(2,1)S(1)}, u32[]{:S(2)}, u32[]{:S(2)}) collective-permute-start(bf16[152,128]{1,0:T(8,128)(2,1)S(1)} %pack.1), channel_id=1, source_target_pairs={{0,8},{1,9},{2,10},{3,11},{4,12},{5,13},{6,14},{7,15},{8,0},{9,1},... | collective-permute-start | bytes 116744 | tf_op jit(solution)/shard_map/gather_line/ppermute | solution.py:456
  6.4 4.9 %collective-permute-start = (bf16[152,128]{1,0:T(8,128)(2,1)S(1)}, bf16[152,128]{1,0:T(8,128)(2,1)S(1)}, u32[]{:S(2)}, u32[]{:S(2)}) collective-permute-start(bf16[152,128]{1,0:T(8,128)(2,1)S(1)} %pack.1), channel_id=1, source_target_pairs={{0,4},{1,5},{2,6},{3,7},{4,0},{5,1},{6,2},{7,3},{8,12},{9,13},{10,... | collective-permute-start | bytes 116744 | tf_op jit(solution)/shard_map/gather_line/ppermute | solution.py:456
  7.0 0.7 %copy-start.3 = (s32[512]{0:T(512)S(1)}, s32[512]{0:T(512)}, u32[]{:S(2)}) copy-start(s32[512]{0:T(512)} %param.7) | copy-start | bytes 6148
  11.3 5.3 %collective-permute-start.3 = (bf16[4,152,128]{2,1,0:T(8,128)(2,1)S(1)}, bf16[4,152,128]{2,1,0:T(8,128)(2,1)S(1)}, u32[]{:S(2)}, u32[]{:S(2)}) collective-permute-start(bf16[4,152,128]{2,1,0:T(8,128)(2,1)S(1)} %pad_maximum_fusion.x0_ref), channel_id=1, source_target_pairs={{0,2},{1,3},{2,0},{3,1},{4,6},{5,7},{6,4},{7,5},{8,10},{9,11},{10,... | collective-permute-start | bytes 466952 | tf_op jit(solution)/shard_map/gather_plane/ppermute | solution.py:456
  14.7 2.1 %collective-permute-start.4 = (bf16[4,152,128]{2,1,0:T(8,128)(2,1)S(1)}, bf16[4,152,128]{2,1,0:T(8,128)(2,1)S(1)}, u32[]{:S(2)}, u32[]{:S(2)}) collective-permute-start(bf16[4,152,128]{2,1,0:T(8,128)(2,1)S(1)} %pad_maximum_fusion.x0_ref), channel_id=1, source_target_pairs={{0,1},{1,0},{2,3},{3,2},{4,5},{5,4},{6,7},{7,6},{8,9},{9,8},{10,11... | collective-permute-start | bytes 466952 | tf_op jit(solution)/shard_map/gather_plane/ppermute | solution.py:456
  16.6 1.4 %collective-permute-start.5 = (bf16[4,152,128]{2,1,0:T(8,128)(2,1)S(1)}, bf16[4,152,128]{2,1,0:T(8,128)(2,1)S(1)}, u32[]{:S(2)}, u32[]{:S(2)}) collective-permute-start(bf16[4,152,128]{2,1,0:T(8,128)(2,1)S(1)} %collective-permute-done.3.x1_ref), channel_id=1, source_target_pairs={{0,1},{1,0},{2,3},{3,2},{4,5},{5,4},{6,7},{7,6},{8,9},{9,8},{10,11... | collective-permute-start | bytes 466952 | tf_op jit(solution)/shard_map/gather_plane/ppermute | solution.py:456
  23.5 1.4 %collective-permute-start.7 = (bf16[4,152,128]{2,1,0:T(8,128)(2,1)S(1)}, bf16[4,152,128]{2,1,0:T(8,128)(2,1)S(1)}, u32[]{:S(2)}, u32[]{:S(2)}) collective-permute-start(bf16[4,152,128]{2,1,0:T(8,128)(2,1)S(1)} %get-tuple-element.48), channel_id=1, source_target_pairs={{0,1},{1,0},{2,3},{3,2},{4,5},{5,4},{6,7},{7,6},{8,9},{9,8},{10,11... | collective-permute-start | bytes 466952 | tf_op jit(solution)/shard_map/sum_cores/ppermute | solution.py:456
  24.2 4.9 %collective-permute-start.6 = (bf16[4,152,128]{2,1,0:T(8,128)(2,1)S(1)}, bf16[4,152,128]{2,1,0:T(8,128)(2,1)S(1)}, u32[]{:S(2)}, u32[]{:S(2)}) collective-permute-start(bf16[4,152,128]{2,1,0:T(8,128)(2,1)S(1)} %get-tuple-element.46), channel_id=1, source_target_pairs={{0,1},{1,0},{2,3},{3,2},{4,5},{5,4},{6,7},{7,6},{8,9},{9,8},{10,11... | collective-permute-start | bytes 466952 | tf_op jit(solution)/shard_map/sum_cores/ppermute | solution.py:456
  25.0 4.1 %collective-permute-start.8 = (bf16[152,128]{1,0:T(8,128)(2,1)S(1)}, bf16[152,128]{1,0:T(8,128)(2,1)S(1)}, u32[]{:S(2)}, u32[]{:S(2)}) collective-permute-start(bf16[152,128]{1,0:T(8,128)(2,1)S(1)} %get-tuple-element.49), channel_id=1, source_target_pairs={{0,2},{1,3},{2,0},{3,1},{4,6},{5,7},{6,4},{7,5},{8,10},{9,11},{10,... | collective-permute-start | bytes 116744 | tf_op jit(solution)/shard_map/sum_plane/ppermute | solution.py:456
  26.6 5.1 %collective-permute-start.10 = (bf16[152,128]{1,0:T(8,128)(2,1)S(1)}, bf16[152,128]{1,0:T(8,128)(2,1)S(1)}, u32[]{:S(2)}, u32[]{:S(2)}) collective-permute-start(bf16[152,128]{1,0:T(8,128)(2,1)S(1)} %get-tuple-element.50), channel_id=1, source_target_pairs={{0,2},{1,3},{2,0},{3,1},{4,6},{5,7},{6,4},{7,5},{8,10},{9,11},{10,... | collective-permute-start | bytes 116744 | tf_op jit(solution)/shard_map/sum_plane/ppermute | solution.py:456
  27.1 4.9 %collective-permute-start.12 = (bf16[152,128]{1,0:T(8,128)(2,1)S(1)}, bf16[152,128]{1,0:T(8,128)(2,1)S(1)}, u32[]{:S(2)}, u32[]{:S(2)}) collective-permute-start(bf16[152,128]{1,0:T(8,128)(2,1)S(1)} %get-tuple-element.51), channel_id=1, source_target_pairs={{0,2},{1,3},{2,0},{3,1},{4,6},{5,7},{6,4},{7,5},{8,10},{9,11},{10,... | collective-permute-start | bytes 116744 | tf_op jit(solution)/shard_map/sum_plane/ppermute | solution.py:456
  28.6 5.3 %collective-permute-start.14 = (bf16[152,128]{1,0:T(8,128)(2,1)S(1)}, bf16[152,128]{1,0:T(8,128)(2,1)S(1)}, u32[]{:S(2)}, u32[]{:S(2)}) collective-permute-start(bf16[152,128]{1,0:T(8,128)(2,1)S(1)} %get-tuple-element.52), channel_id=1, source_target_pairs={{0,2},{1,3},{2,0},{3,1},{4,6},{5,7},{6,4},{7,5},{8,10},{9,11},{10,... | collective-permute-start | bytes 116744 | tf_op jit(solution)/shard_map/sum_plane/ppermute | solution.py:456
  29.2 5.8 %collective-permute-start.9 = (bf16[152,128]{1,0:T(8,128)(2,1)S(1)}, bf16[152,128]{1,0:T(8,128)(2,1)S(1)}, u32[]{:S(2)}, u32[]{:S(2)}) collective-permute-start(bf16[152,128]{1,0:T(8,128)(2,1)S(1)} %sum_line.4), channel_id=1, source_target_pairs={{0,12},{1,13},{2,14},{3,15},{4,8},{5,9},{6,10},{7,11},{8,4},{9,5},... | collective-permute-start | bytes 116744 | tf_op jit(solution)/shard_map/sum_line/ppermute | solution.py:456
  31.8 4.0 %collective-permute-start.11 = (bf16[152,128]{1,0:T(8,128)(2,1)S(1)}, bf16[152,128]{1,0:T(8,128)(2,1)S(1)}, u32[]{:S(2)}, u32[]{:S(2)}) collective-permute-start(bf16[152,128]{1,0:T(8,128)(2,1)S(1)} %sum_line.5), channel_id=1, source_target_pairs={{0,4},{1,5},{2,6},{3,7},{4,0},{5,1},{6,2},{7,3},{8,12},{9,13},{10,... | collective-permute-start | bytes 116744 | tf_op jit(solution)/shard_map/sum_line/ppermute | solution.py:456
  32.0 4.9 %collective-permute-start.13 = (bf16[152,128]{1,0:T(8,128)(2,1)S(1)}, bf16[152,128]{1,0:T(8,128)(2,1)S(1)}, u32[]{:S(2)}, u32[]{:S(2)}) collective-permute-start(bf16[152,128]{1,0:T(8,128)(2,1)S(1)} %sum_line.6), channel_id=1, source_target_pairs={{0,8},{1,9},{2,10},{3,11},{4,12},{5,13},{6,14},{7,15},{8,0},{9,1},... | collective-permute-start | bytes 116744 | tf_op jit(solution)/shard_map/sum_line/ppermute | solution.py:456

commit v3 on v2

--- a/solution.py
+++ b/solution.py
@@ -276,7 +276,7 @@
             tt_ref[t, span, 3 * LANES : 4 * LANES] = jnp.where(use_b, sin_part, 0.0).astype(BF16)
         return carry
 
-    lax.fori_loop(0, half_total // SUB, block, 0)
+    lax.fori_loop(0, half_total // SUB, block, 0, unroll=2)
 
 
 def turn_kernel(half_total, tt_ref, weight_ref, rate_ref, tr_ref, scale_ref, factor_ref):
@@ -289,7 +289,7 @@
             tr_ref[t, lanes, :] = tt_ref[t, :, lanes].T
         return carry
 
-    lax.fori_loop(0, half_total // SUB, block, 0)
+    lax.fori_loop(0, half_total // SUB, block, 0, unroll=2)
     weight = jnp.broadcast_to(weight_ref[...], (LANES, lat_total)).T
     scale = weight / row_length(iota((lat_total, LANES), 0), lat_total).astype(F32)
     keep = iota((SUB, LANES), 1) % SUB == iota((SUB, LANES), 0)

time: 38.1 us -> 38.1 us (level)
  waiting for transfers between devices: 6.22 us -> 6.61 us
    ppermute x15, waiting for transfers between devices: 6.22 us -> 6.61 us  [across(): return lax.ppermute(x, 'lat', [(i, i ^ step) for i in range(groups)])]
where the time goes in v3:
time: 38.1 us; the launch traced here: 37.9 us
  starting transfers between devices  16.9 us (44%)
  Pallas kernels  10.9 us (29%)
  waiting for transfers between devices  6.61 us (17%)
  local copies, waits for them, and re-layouts  3.38 us (9%)
    ppermute x15, starting transfers between devices, across(): return lax.ppermute(x, 'lat', [(i, i ^ step) for i in range(groups)])  16.9 us
    ppermute x15, waiting for transfers between devices, across(): return lax.ppermute(x, 'lat', [(i, i ^ step) for i in range(groups)])  6.61 us
    pallas_call x1, Pallas kernels, transform_call(): pl.pallas_call(main_kernel, out_shape=[jax.ShapeDtypeStruct((line, lines,...  5.55 us
    pallas_call x1, Pallas kernels, short_rows_body(): kernel_call(functools.partial(table_kernel, half_total, cols, waves), (sh...  2.2 us
    slice x1, local copies, waits for them, and re-layouts, short_rows_body(): half_legendre = legendre[:slots]  1.78 us
    unnamed x8, local copies, waits for them, and re-layouts  1.6 us
    pallas_call x1, Pallas kernels, short_rows_body(): kernel_call(functools.partial(turn_kernel, half_total), (shape((blocks, 4...  1.19 us
    pallas_call x1, Pallas kernels, short_rows_body(): kernel_call(unpack_kernel, shape((cols, channels, half_total), BF16), [wh...  0.98 us
  transfers between devices with their start and end apart: 15, of which 7 were waited for; matrix products, arithmetic and copies ran while one was open for 5% of the time, Pallas kernels for 11%

profile of v3, /device:TPU:0, one launch (start us, length us, event | category | flops | bytes accessed | tf_op | source)
XLA Modules:
  0.0 37.9 jit_solution(12356306798886618173)
XLA Ops:
  0.0 0.9 %copy-done = bf16[16,64,19]{1,0,2:T(8,128)(2,1)S(1)} copy-done((bf16[16,64,19]{1,0,2:T(8,128)(2,1)S(1)}, bf16[16,64,19]{1,0,2:T(8,128)(2,1)}, u32[]{:S(2)}) %copy-start) | copy-done | bytes 38936
  1.3 5.1 %collective-permute-start.2 = (bf16[152,128]{1,0:T(8,128)(2,1)S(1)}, bf16[152,128]{1,0:T(8,128)(2,1)S(1)}, u32[]{:S(2)}, u32[]{:S(2)}) collective-permute-start(bf16[152,128]{1,0:T(8,128)(2,1)S(1)} %pack.1), channel_id=1, source_target_pairs={{0,12},{1,13},{2,14},{3,15},{4,8},{5,9},{6,10},{7,11},{8,4},{9,5},... | collective-permute-start | bytes 116744 | tf_op jit(solution)/shard_map/gather_line/ppermute | solution.py:456
  6.4 0.6 %collective-permute-start = (bf16[152,128]{1,0:T(8,128)(2,1)S(1)}, bf16[152,128]{1,0:T(8,128)(2,1)S(1)}, u32[]{:S(2)}, u32[]{:S(2)}) collective-permute-start(bf16[152,128]{1,0:T(8,128)(2,1)S(1)} %pack.1), channel_id=1, source_target_pairs={{0,4},{1,5},{2,6},{3,7},{4,0},{5,1},{6,2},{7,3},{8,12},{9,13},{10,... | collective-permute-start | bytes 116744 | tf_op jit(solution)/shard_map/gather_line/ppermute | solution.py:456
  7.0 0.7 %copy-done.3 = s32[512]{0:T(512)S(1)} copy-done((s32[512]{0:T(512)S(1)}, s32[512]{0:T(512)}, u32[]{:S(2)}) %copy-start.3) | copy-done | bytes 2072
  7.7 2.2 %tables.1 = (bf16[8,304,512]{2,1,0:T(8,128)(2,1)S(1)}, f32[16,128]{1,0:T(8,128)S(1)}) custom-call(s32[1]{0:T(128)} %bitcast.1.device_ref, s32[1,512]{1,0:T(1,128)S(1)} %bitcast.14), custom_call_target="tpu_custom_call" | custom-call | flops 12582912 | bytes 3145728 | tf_op jit(solution)/shard_map/tables/pallas_call | solution.py:462
  9.9 1.3 %collective-permute-done.1 = bf16[152,128]{1,0:T(8,128)(2,1)S(1)} collective-permute-done((bf16[152,128]{1,0:T(8,128)(2,1)S(1)}, bf16[152,128]{1,0:T(8,128)(2,1)S(1)}, u32[]{:S(2)}, u32[]{:S(2)}) %collective-permute-start.1) | collective-permute-done | bytes 38944 | tf_op jit(solution)/shard_map/gather_line/ppermute | solution.py:456
  11.3 1.6 %collective-permute-start.3 = (bf16[4,152,128]{2,1,0:T(8,128)(2,1)S(1)}, bf16[4,152,128]{2,1,0:T(8,128)(2,1)S(1)}, u32[]{:S(2)}, u32[]{:S(2)}) collective-permute-start(bf16[4,152,128]{2,1,0:T(8,128)(2,1)S(1)} %pad_maximum_fusion.x0_ref), channel_id=1, source_target_pairs={{0,2},{1,3},{2,0},{3,1},{4,6},{5,7},{6,4},{7,5},{8,10},{9,11},{10,... | collective-permute-start | bytes 466952 | tf_op jit(solution)/shard_map/gather_plane/ppermute | solution.py:456
  12.9 1.8 %slice.3.leg_ref = bf16[16,512,128]{2,1,0:T(8,128)(2,1)S(1)} slice(bf16[32,512,128]{2,1,0:T(8,128)(2,1)} %param.8), slice={[0:16], [0:512], [0:128]} | slice | bytes 4194304 | tf_op jit(solution)/shard_map/gather_plane/slice | solution.py:486
  14.8 1.2 %gather_plane.1 = (bf16[8,512,304]{2,1,0:T(8,128)(2,1)S(1)}, f32[16,8,128]{2,1,0:T(8,128)S(1)}, f32[512,128]{1,0:T(8,128)S(1)}) custom-call(bf16[8,304,512]{2,1,0:T(8,128)(2,1)S(1)} %get-tuple-element.31.tt_ref, f32[1,128]{1,0:T(1,128)S(1)} %bitcast.12, f32[1,4]{1,0:T(1,128)S(1)} %bitcast.13), custom_call_target="tpu_custom_call" | custom-call | flops 12582912 | bytes 6291456 | tf_op jit(solution)/shard_map/gather_plane/pallas_call | solution.py:475
  16.0 0.6 %collective-permute-done.3.x1_ref = bf16[4,152,128]{2,1,0:T(8,128)(2,1)S(1)} collective-permute-done((bf16[4,152,128]{2,1,0:T(8,128)(2,1)S(1)}, bf16[4,152,128]{2,1,0:T(8,128)(2,1)S(1)}, u32[]{:S(2)}, u32[]{:S(2)}) %collective-permute-start.3) | collective-permute-done | bytes 155680 | tf_op jit(solution)/shard_map/gather_plane/ppermute | solution.py:456
  16.6 1.4 %collective-permute-done.5.x3_ref = bf16[4,152,128]{2,1,0:T(8,128)(2,1)S(1)} collective-permute-done((bf16[4,152,128]{2,1,0:T(8,128)(2,1)S(1)}, bf16[4,152,128]{2,1,0:T(8,128)(2,1)S(1)}, u32[]{:S(2)}, u32[]{:S(2)}) %collective-permute-start.5) | collective-permute-done | bytes 155680 | tf_op jit(solution)/shard_map/gather_plane/ppermute | solution.py:456
  18.0 5.5 %transform.1 = (bf16[4,152,128]{2,1,0:T(8,128)(2,1)S(1)}, bf16[4,152,128]{2,1,0:T(8,128)(2,1)S(1)}, bf16[8,512,128]{2,1,0:T(8,128)(2,1)S(1)}) custom-call(bf16[4,152,128]{2,1,0:T(8,128)(2,1)S(1)} %pad_maximum_fusion.x0_ref, bf16[4,152,128]{2,1,0:T(8,128)(2,1)S(1)} %collective-permute-done.3.x1_ref, bf16[4,152,128]{2,1,0:T(8,128)(2,1)S(1)} %collective-permute-done.4.x2_ref, ...), custom_call_target="tpu_custom_call" | custom-call | tf_op jit(solution)/shard_map/transform/pallas_call | solution.py:424
  23.7 0.5 %sum_cores.2 = (bf16[4,152,128]{2,1,0:T(8,128)(2,1)S(1)}, bf16[4,152,128]{2,1,0:T(8,128)(2,1)S(1)}) custom-call(bf16[8,304,512]{2,1,0:T(8,128)(2,1)S(1)} %get-tuple-element.31.tt_ref, bf16[8,512,128]{2,1,0:T(8,128)(2,1)S(1)} %get-tuple-element.44.rhs_ref), custom_call_target="tpu_custom_call" | custom-call | tf_op jit(solution)/shard_map/sum_cores/pallas_call | solution.py:495
  24.2 0.4 %collective-permute-start.6 = (bf16[4,152,128]{2,1,0:T(8,128)(2,1)S(1)}, bf16[4,152,128]{2,1,0:T(8,128)(2,1)S(1)}, u32[]{:S(2)}, u32[]{:S(2)}) collective-permute-start(bf16[4,152,128]{2,1,0:T(8,128)(2,1)S(1)} %get-tuple-element.46), channel_id=1, source_target_pairs={{0,1},{1,0},{2,3},{3,2},{4,5},{5,4},{6,7},{7,6},{8,9},{9,8},{10,11... | collective-permute-start | bytes 466952 | tf_op jit(solution)/shard_map/sum_cores/ppermute | solution.py:456
  25.0 1.6 %collective-permute-start.8 = (bf16[152,128]{1,0:T(8,128)(2,1)S(1)}, bf16[152,128]{1,0:T(8,128)(2,1)S(1)}, u32[]{:S(2)}, u32[]{:S(2)}) collective-permute-start(bf16[152,128]{1,0:T(8,128)(2,1)S(1)} %get-tuple-element.49), channel_id=1, source_target_pairs={{0,2},{1,3},{2,0},{3,1},{4,6},{5,7},{6,4},{7,5},{8,10},{9,11},{10,... | collective-permute-start | bytes 116744 | tf_op jit(solution)/shard_map/sum_plane/ppermute | solution.py:456
  26.6 0.5 %collective-permute-start.10 = (bf16[152,128]{1,0:T(8,128)(2,1)S(1)}, bf16[152,128]{1,0:T(8,128)(2,1)S(1)}, u32[]{:S(2)}, u32[]{:S(2)}) collective-permute-start(bf16[152,128]{1,0:T(8,128)(2,1)S(1)} %get-tuple-element.50), channel_id=1, source_target_pairs={{0,2},{1,3},{2,0},{3,1},{4,6},{5,7},{6,4},{7,5},{8,10},{9,11},{10,... | collective-permute-start | bytes 116744 | tf_op jit(solution)/shard_map/sum_plane/ppermute | solution.py:456
  27.1 1.5 %collective-permute-start.12 = (bf16[152,128]{1,0:T(8,128)(2,1)S(1)}, bf16[152,128]{1,0:T(8,128)(2,1)S(1)}, u32[]{:S(2)}, u32[]{:S(2)}) collective-permute-start(bf16[152,128]{1,0:T(8,128)(2,1)S(1)} %get-tuple-element.51), channel_id=1, source_target_pairs={{0,2},{1,3},{2,0},{3,1},{4,6},{5,7},{6,4},{7,5},{8,10},{9,11},{10,... | collective-permute-start | bytes 116744 | tf_op jit(solution)/shard_map/sum_plane/ppermute | solution.py:456
  28.6 0.5 %collective-permute-start.14 = (bf16[152,128]{1,0:T(8,128)(2,1)S(1)}, bf16[152,128]{1,0:T(8,128)(2,1)S(1)}, u32[]{:S(2)}, u32[]{:S(2)}) collective-permute-start(bf16[152,128]{1,0:T(8,128)(2,1)S(1)} %get-tuple-element.52), channel_id=1, source_target_pairs={{0,2},{1,3},{2,0},{3,1},{4,6},{5,7},{6,4},{7,5},{8,10},{9,11},{10,... | collective-permute-start | bytes 116744 | tf_op jit(solution)/shard_map/sum_plane/ppermute | solution.py:456
  29.2 2.5 %collective-permute-start.9 = (bf16[152,128]{1,0:T(8,128)(2,1)S(1)}, bf16[152,128]{1,0:T(8,128)(2,1)S(1)}, u32[]{:S(2)}, u32[]{:S(2)}) collective-permute-start(bf16[152,128]{1,0:T(8,128)(2,1)S(1)} %sum_line.4), channel_id=1, source_target_pairs={{0,12},{1,13},{2,14},{3,15},{4,8},{5,9},{6,10},{7,11},{8,4},{9,5},... | collective-permute-start | bytes 116744 | tf_op jit(solution)/shard_map/sum_line/ppermute | solution.py:456
  32.0 1.9 %collective-permute-start.13 = (bf16[152,128]{1,0:T(8,128)(2,1)S(1)}, bf16[152,128]{1,0:T(8,128)(2,1)S(1)}, u32[]{:S(2)}, u32[]{:S(2)}) collective-permute-start(bf16[152,128]{1,0:T(8,128)(2,1)S(1)} %sum_line.6), channel_id=1, source_target_pairs={{0,8},{1,9},{2,10},{3,11},{4,12},{5,13},{6,14},{7,15},{8,0},{9,1},... | collective-permute-start | bytes 116744 | tf_op jit(solution)/shard_map/sum_line/ppermute | solution.py:456
  34.0 1.0 %collective-permute-done.9.refs_0_ = bf16[152,128]{1,0:T(8,128)(2,1)S(1)} collective-permute-done((bf16[152,128]{1,0:T(8,128)(2,1)S(1)}, bf16[152,128]{1,0:T(8,128)(2,1)S(1)}, u32[]{:S(2)}, u32[]{:S(2)}) %collective-permute-start.9) | collective-permute-done | bytes 38944 | tf_op jit(solution)/shard_map/sum_line/ppermute | solution.py:456
  35.0 0.7 %collective-permute-done.11.refs_1_ = bf16[152,128]{1,0:T(8,128)(2,1)S(1)} collective-permute-done((bf16[152,128]{1,0:T(8,128)(2,1)S(1)}, bf16[152,128]{1,0:T(8,128)(2,1)S(1)}, u32[]{:S(2)}, u32[]{:S(2)}) %collective-permute-start.11) | collective-permute-done | bytes 38944 | tf_op jit(solution)/shard_map/sum_line/ppermute | solution.py:456
  35.7 1.2 %collective-permute-done.13.refs_2_ = bf16[152,128]{1,0:T(8,128)(2,1)S(1)} collective-permute-done((bf16[152,128]{1,0:T(8,128)(2,1)S(1)}, bf16[152,128]{1,0:T(8,128)(2,1)S(1)}, u32[]{:S(2)}, u32[]{:S(2)}) %collective-permute-start.13) | collective-permute-done | bytes 38944 | tf_op jit(solution)/shard_map/sum_line/ppermute | solution.py:456
  36.9 1.0 %unpack.1 = bf16[19,16,64]{2,1,0:T(8,128)(2,1)} custom-call(bf16[152,128]{1,0:T(8,128)(2,1)S(1)} %collective-permute-done.9.refs_0_, bf16[152,128]{1,0:T(8,128)(2,1)S(1)} %collective-permute-done.11.refs_1_, bf16[152,128]{1,0:T(8,128)(2,1)S(1)} %collective-permute-done.13.refs_2_, bf16[152,128]{1,0:T(8,128)(2,1)S(1)} %sum_line.7.refs_3_), custom_call_target="tpu_custom_call" | custom-call | tf_op jit(solution)/shard_map/unpack/pallas_call | solution.py:507
  (27 shorter events, 1.4 us)
Async XLA Ops:
  0.0 14.7 %copy-start.2 = (f32[4]{0:T(128)S(1)}, f32[4]{0:T(128)}, u32[]{:S(2)}) copy-start(f32[4]{0:T(128)} %param.9) | copy-start | bytes 52
  0.0 14.7 %copy-start.1 = (f32[128]{0:T(128)S(1)}, f32[128]{0:T(128)}, u32[]{:S(2)}) copy-start(f32[128]{0:T(128)} %param.6) | copy-start | bytes 1540
  0.0 0.9 %copy-start = (bf16[16,64,19]{1,0,2:T(8,128)(2,1)S(1)}, bf16[16,64,19]{1,0,2:T(8,128)(2,1)}, u32[]{:S(2)}) copy-start(bf16[16,64,19]{1,0,2:T(8,128)(2,1)} %param.5) | copy-start | bytes 116740
  1.3 8.6 %collective-permute-start.2 = (bf16[152,128]{1,0:T(8,128)(2,1)S(1)}, bf16[152,128]{1,0:T(8,128)(2,1)S(1)}, u32[]{:S(2)}, u32[]{:S(2)}) collective-permute-start(bf16[152,128]{1,0:T(8,128)(2,1)S(1)} %pack.1), channel_id=1, source_target_pairs={{0,12},{1,13},{2,14},{3,15},{4,8},{5,9},{6,10},{7,11},{8,4},{9,5},... | collective-permute-start | bytes 116744 | tf_op jit(solution)/shard_map/gather_line/ppermute | solution.py:456
  6.4 4.9 %collective-permute-start.1 = (bf16[152,128]{1,0:T(8,128)(2,1)S(1)}, bf16[152,128]{1,0:T(8,128)(2,1)S(1)}, u32[]{:S(2)}, u32[]{:S(2)}) collective-permute-start(bf16[152,128]{1,0:T(8,128)(2,1)S(1)} %pack.1), channel_id=1, source_target_pairs={{0,8},{1,9},{2,10},{3,11},{4,12},{5,13},{6,14},{7,15},{8,0},{9,1},... | collective-permute-start | bytes 116744 | tf_op jit(solution)/shard_map/gather_line/ppermute | solution.py:456
  6.4 4.9 %collective-permute-start = (bf16[152,128]{1,0:T(8,128)(2,1)S(1)}, bf16[152,128]{1,0:T(8,128)(2,1)S(1)}, u32[]{:S(2)}, u32[]{:S(2)}) collective-permute-start(bf16[152,128]{1,0:T(8,128)(2,1)S(1)} %pack.1), channel_id=1, source_target_pairs={{0,4},{1,5},{2,6},{3,7},{4,0},{5,1},{6,2},{7,3},{8,12},{9,13},{10,... | collective-permute-start | bytes 116744 | tf_op jit(solution)/shard_map/gather_line/ppermute | solution.py:456
  7.0 0.7 %copy-start.3 = (s32[512]{0:T(512)S(1)}, s32[512]{0:T(512)}, u32[]{:S(2)}) copy-start(s32[512]{0:T(512)} %param.7) | copy-start | bytes 6148
  11.3 5.3 %collective-permute-start.3 = (bf16[4,152,128]{2,1,0:T(8,128)(2,1)S(1)}, bf16[4,152,128]{2,1,0:T(8,128)(2,1)S(1)}, u32[]{:S(2)}, u32[]{:S(2)}) collective-permute-start(bf16[4,152,128]{2,1,0:T(8,128)(2,1)S(1)} %pad_maximum_fusion.x0_ref), channel_id=1, source_target_pairs={{0,2},{1,3},{2,0},{3,1},{4,6},{5,7},{6,4},{7,5},{8,10},{9,11},{10,... | collective-permute-start | bytes 466952 | tf_op jit(solution)/shard_map/gather_plane/ppermute | solution.py:456
  14.7 1.9 %collective-permute-start.4 = (bf16[4,152,128]{2,1,0:T(8,128)(2,1)S(1)}, bf16[4,152,128]{2,1,0:T(8,128)(2,1)S(1)}, u32[]{:S(2)}, u32[]{:S(2)}) collective-permute-start(bf16[4,152,128]{2,1,0:T(8,128)(2,1)S(1)} %pad_maximum_fusion.x0_ref), channel_id=1, source_target_pairs={{0,1},{1,0},{2,3},{3,2},{4,5},{5,4},{6,7},{7,6},{8,9},{9,8},{10,11... | collective-permute-start | bytes 466952 | tf_op jit(solution)/shard_map/gather_plane/ppermute | solution.py:456
  16.6 1.4 %collective-permute-start.5 = (bf16[4,152,128]{2,1,0:T(8,128)(2,1)S(1)}, bf16[4,152,128]{2,1,0:T(8,128)(2,1)S(1)}, u32[]{:S(2)}, u32[]{:S(2)}) collective-permute-start(bf16[4,152,128]{2,1,0:T(8,128)(2,1)S(1)} %collective-permute-done.3.x1_ref), channel_id=1, source_target_pairs={{0,1},{1,0},{2,3},{3,2},{4,5},{5,4},{6,7},{7,6},{8,9},{9,8},{10,11... | collective-permute-start | bytes 466952 | tf_op jit(solution)/shard_map/gather_plane/ppermute | solution.py:456
  23.5 1.4 %collective-permute-start.7 = (bf16[4,152,128]{2,1,0:T(8,128)(2,1)S(1)}, bf16[4,152,128]{2,1,0:T(8,128)(2,1)S(1)}, u32[]{:S(2)}, u32[]{:S(2)}) collective-permute-start(bf16[4,152,128]{2,1,0:T(8,128)(2,1)S(1)} %get-tuple-element.48), channel_id=1, source_target_pairs={{0,1},{1,0},{2,3},{3,2},{4,5},{5,4},{6,7},{7,6},{8,9},{9,8},{10,11... | collective-permute-start | bytes 466952 | tf_op jit(solution)/shard_map/sum_cores/ppermute | solution.py:456
  24.2 4.9 %collective-permute-start.6 = (bf16[4,152,128]{2,1,0:T(8,128)(2,1)S(1)}, bf16[4,152,128]{2,1,0:T(8,128)(2,1)S(1)}, u32[]{:S(2)}, u32[]{:S(2)}) collective-permute-start(bf16[4,152,128]{2,1,0:T(8,128)(2,1)S(1)} %get-tuple-element.46), channel_id=1, source_target_pairs={{0,1},{1,0},{2,3},{3,2},{4,5},{5,4},{6,7},{7,6},{8,9},{9,8},{10,11... | collective-permute-start | bytes 466952 | tf_op jit(solution)/shard_map/sum_cores/ppermute | solution.py:456
  25.0 4.1 %collective-permute-start.8 = (bf16[152,128]{1,0:T(8,128)(2,1)S(1)}, bf16[152,128]{1,0:T(8,128)(2,1)S(1)}, u32[]{:S(2)}, u32[]{:S(2)}) collective-permute-start(bf16[152,128]{1,0:T(8,128)(2,1)S(1)} %get-tuple-element.49), channel_id=1, source_target_pairs={{0,2},{1,3},{2,0},{3,1},{4,6},{5,7},{6,4},{7,5},{8,10},{9,11},{10,... | collective-permute-start | bytes 116744 | tf_op jit(solution)/shard_map/sum_plane/ppermute | solution.py:456
  26.6 5.0 %collective-permute-start.10 = (bf16[152,128]{1,0:T(8,128)(2,1)S(1)}, bf16[152,128]{1,0:T(8,128)(2,1)S(1)}, u32[]{:S(2)}, u32[]{:S(2)}) collective-permute-start(bf16[152,128]{1,0:T(8,128)(2,1)S(1)} %get-tuple-element.50), channel_id=1, source_target_pairs={{0,2},{1,3},{2,0},{3,1},{4,6},{5,7},{6,4},{7,5},{8,10},{9,11},{10,... | collective-permute-start | bytes 116744 | tf_op jit(solution)/shard_map/sum_plane/ppermute | solution.py:456
  27.1 4.9 %collective-permute-start.12 = (bf16[152,128]{1,0:T(8,128)(2,1)S(1)}, bf16[152,128]{1,0:T(8,128)(2,1)S(1)}, u32[]{:S(2)}, u32[]{:S(2)}) collective-permute-start(bf16[152,128]{1,0:T(8,128)(2,1)S(1)} %get-tuple-element.51), channel_id=1, source_target_pairs={{0,2},{1,3},{2,0},{3,1},{4,6},{5,7},{6,4},{7,5},{8,10},{9,11},{10,... | collective-permute-start | bytes 116744 | tf_op jit(solution)/shard_map/sum_plane/ppermute | solution.py:456
  28.6 5.3 %collective-permute-start.14 = (bf16[152,128]{1,0:T(8,128)(2,1)S(1)}, bf16[152,128]{1,0:T(8,128)(2,1)S(1)}, u32[]{:S(2)}, u32[]{:S(2)}) collective-permute-start(bf16[152,128]{1,0:T(8,128)(2,1)S(1)} %get-tuple-element.52), channel_id=1, source_target_pairs={{0,2},{1,3},{2,0},{3,1},{4,6},{5,7},{6,4},{7,5},{8,10},{9,11},{10,... | collective-permute-start | bytes 116744 | tf_op jit(solution)/shard_map/sum_plane/ppermute | solution.py:456
  29.2 5.8 %collective-permute-start.9 = (bf16[152,128]{1,0:T(8,128)(2,1)S(1)}, bf16[152,128]{1,0:T(8,128)(2,1)S(1)}, u32[]{:S(2)}, u32[]{:S(2)}) collective-permute-start(bf16[152,128]{1,0:T(8,128)(2,1)S(1)} %sum_line.4), channel_id=1, source_target_pairs={{0,12},{1,13},{2,14},{3,15},{4,8},{5,9},{6,10},{7,11},{8,4},{9,5},... | collective-permute-start | bytes 116744 | tf_op jit(solution)/shard_map/sum_line/ppermute | solution.py:456
  31.7 4.0 %collective-permute-start.11 = (bf16[152,128]{1,0:T(8,128)(2,1)S(1)}, bf16[152,128]{1,0:T(8,128)(2,1)S(1)}, u32[]{:S(2)}, u32[]{:S(2)}) collective-permute-start(bf16[152,128]{1,0:T(8,128)(2,1)S(1)} %sum_line.5), channel_id=1, source_target_pairs={{0,4},{1,5},{2,6},{3,7},{4,0},{5,1},{6,2},{7,3},{8,12},{9,13},{10,... | collective-permute-start | bytes 116744 | tf_op jit(solution)/shard_map/sum_line/ppermute | solution.py:456
  32.0 4.9 %collective-permute-start.13 = (bf16[152,128]{1,0:T(8,128)(2,1)S(1)}, bf16[152,128]{1,0:T(8,128)(2,1)S(1)}, u32[]{:S(2)}, u32[]{:S(2)}) collective-permute-start(bf16[152,128]{1,0:T(8,128)(2,1)S(1)} %sum_line.6), channel_id=1, source_target_pairs={{0,8},{1,9},{2,10},{3,11},{4,12},{5,13},{6,14},{7,15},{8,0},{9,1},... | collective-permute-start | bytes 116744 | tf_op jit(solution)/shard_map/sum_line/ppermute | solution.py:456
